TPU v7x, 32 devices: a whole 2x2x4 slice. The times are simulated.
32 devices in a mesh: dp: 8 (over y, x, core), tensor: 4 (over z).
Axes of the slice: x: 2, y: 2, z: 4, core: 2. Of those that a mesh axis runs over, the one named last changes fastest.
Arguments:
- inputs: bfloat16 [1024, 16, 768], P('tensor', 'dp'), may hold values from -6 to 6
- qkv_weight: bfloat16 [768, 3, 768], P(None, None, 'tensor'), may hold values from -0.21875 to 0.21875
- qv_bias: bfloat16 [2, 768], P(None, 'tensor'), may hold values from -1.796875 to 1.796875
- out_weight: bfloat16 [768, 768], P('tensor'), may hold values from -0.875 to 0.875
- out_bias: bfloat16 [768], replicated, may hold values from -1.796875 to 1.796875
- first_gain: bfloat16 [768], replicated, may hold values from 0.5 to 1.5
- first_shift: bfloat16 [768], replicated, may hold values from -1.796875 to 1.796875
- first_layer_weight: bfloat16 [768, 3072], P(None, 'tensor'), may hold values from -0.21875 to 0.21875
- first_layer_bias: bfloat16 [3072], P('tensor'), may hold values from -1.796875 to 1.796875
- second_layer_weight: bfloat16 [3072, 768], P('tensor'), may hold values from -0.15625 to 0.15625
- second_layer_bias: bfloat16 [768], replicated, may hold values from -1.796875 to 1.796875
- second_gain: bfloat16 [768], replicated, may hold values from 0.5 to 1.5
- second_shift: bfloat16 [768], replicated, may hold values from -1.796875 to 1.796875
- cluster_order: int32 [16, 12, 1024], P('dp', 'tensor'), may hold values from 0 to 1023, each once within a row
- masked_rows: int32 [16, 154], P('dp'), may hold values from 0 to 1023, as said below
- masked_grad: bfloat16 [16, 154, 768], P('dp'), may hold values from -6 to 6
Outputs:
- outputs: bfloat16 [1024, 16, 768], P('tensor', 'dp')
- grad_inputs: float32 [1024, 16, 768], P('tensor', 'dp')
- grad_qkvweight: float32 [768, 3, 768], P(None, None, 'tensor')
- grad_qvbias: float32 [2, 768], P(None, 'tensor')
- grad_outweight: float32 [768, 768], P('tensor')
- grad_outbias: float32 [768], replicated
- grad_firstgain: float32 [768], replicated
- grad_firstshift: float32 [768], replicated
- grad_upweight: float32 [768, 3072], P(None, 'tensor')
- grad_upbias: float32 [3072], P('tensor')
- grad_downweight: float32 [3072, 768], P('tensor')
- grad_downbias: float32 [768], replicated
- grad_secondgain: float32 [768], replicated
- grad_secondshift: float32 [768], replicated
Inputs may be any that keep to these rules, and one draw needn't show every extreme that they name: cluster_order[s, h] lists every position of sequence s exactly once. `masked_rows`: the positions of one sequence are distinct.
All inputs are finite; a program needn't handle non-finite values.
Results may differ from a plain program's by a relative error of at most 0.017.
Values may be sent and summed in bfloat16 or wider, within the bound.
A program may use at most 128 MiB of HBM per device.

v0:
```python
import math

import jax
import jax.numpy as jnp
from jax import lax
from jax.sharding import PartitionSpec as P

HD = 64
C = 128


NORM_EPS = 1e-05


def layer_norm(values, gain, shift):
    center = values - jnp.mean(values, axis=-1, keepdims=True)
    spread = jnp.mean(center * center, axis=-1, keepdims=True)
    return center * lax.rsqrt(spread + NORM_EPS) * gain + shift


def gelu_exact(values):
    return jax.nn.gelu(values, approximate=False)


def sort_heads(values, ordering):
    return jax.vmap(lambda block, picks: jnp.take(block, picks, axis=0))(values, ordering)


def unsort_heads(values, ordering):
    return jax.vmap(lambda block, picks: jnp.zeros_like(block).at[picks].set(block))(
        values, ordering
    )


def clusters(values):
    return values.reshape(values.shape[0], values.shape[1] // C, C, HD)


def cluster_scores(q_sorted, k_sorted):
    score_scale = 1.0 / math.sqrt(HD)
    return (
        jnp.einsum("hnqd,hnkd->hnqk", q_sorted, k_sorted, preferred_element_type=jnp.float32)
        * score_scale
    )


def attend_forward(packed):
    query, keyed, valued, ordering = packed
    q_sorted = clusters(sort_heads(query, ordering))
    k_sorted = clusters(sort_heads(keyed, ordering))
    v_sorted = clusters(sort_heads(valued, ordering))
    scores = cluster_scores(q_sorted, k_sorted)
    top = jnp.max(scores, axis=-1, keepdims=True)
    expo = jnp.exp(scores - top)
    total = jnp.sum(expo, axis=-1, keepdims=True)
    probs = (expo / total).astype(jnp.bfloat16)
    mixed = jnp.einsum("hnqk,hnkd->hnqd", probs, v_sorted, preferred_element_type=jnp.float32)
    mixed = unsort_heads(mixed.reshape(query.shape), ordering)
    return (mixed, top + jnp.log(total))


def attend_backward(packed):
    query, keyed, valued, upstream, ordering, logsum = packed
    score_scale = 1.0 / math.sqrt(HD)
    q_sorted = clusters(sort_heads(query, ordering))
    k_sorted = clusters(sort_heads(keyed, ordering))
    v_sorted = clusters(sort_heads(valued, ordering))
    up_sorted = clusters(sort_heads(upstream, ordering))
    probs = jnp.exp(cluster_scores(q_sorted, k_sorted) - logsum)
    probs_low = probs.astype(jnp.bfloat16)
    d_value = jnp.einsum(
        "hnqk,hnqd->hnkd", probs_low, up_sorted, preferred_element_type=jnp.float32
    )
    d_probs = jnp.einsum("hnqd,hnkd->hnqk", up_sorted, v_sorted, preferred_element_type=jnp.float32)
    center = jnp.sum(probs * d_probs, axis=-1, keepdims=True)
    d_scores = (probs * (d_probs - center)).astype(jnp.bfloat16)
    d_query = (
        jnp.einsum("hnqk,hnkd->hnqd", d_scores, k_sorted, preferred_element_type=jnp.float32)
        * score_scale
    )
    d_keyed = (
        jnp.einsum("hnqk,hnqd->hnkd", d_scores, q_sorted, preferred_element_type=jnp.float32)
        * score_scale
    )
    shape_back = query.shape
    d_query = unsort_heads(d_query.reshape(shape_back), ordering)
    d_keyed = unsort_heads(d_keyed.reshape(shape_back), ordering)
    d_value = unsort_heads(d_value.reshape(shape_back), ordering)
    return jnp.stack([d_query, d_keyed, d_value]).astype(jnp.bfloat16)


def shards(
    inputs,
    qkv_weight,
    qv_bias,
    out_weight,
    out_bias,
    first_gain,
    first_shift,
    first_layer_weight,
    first_layer_bias,
    second_layer_weight,
    second_layer_bias,
    second_gain,
    second_shift,
    cluster_order,
    masked_rows,
    masked_grad,
):
    shard = inputs.shape[0]
    seqs = inputs.shape[1]
    width = inputs.shape[2]
    local_width = qkv_weight.shape[2]
    heads = local_width // HD
    length = shard * lax.axis_size("tensor")
    rank = lax.axis_index("tensor")
    weight_flat = qkv_weight.reshape(width, 3 * local_width)
    bias_flat = jnp.concatenate(
        [
            qv_bias[0].astype(jnp.float32),
            jnp.zeros((local_width,), jnp.float32),
            qv_bias[1].astype(jnp.float32),
        ]
    )
    inputs_all = lax.all_gather(inputs, "tensor", axis=0, tiled=True)
    qkv = (
        jnp.einsum("lsd,de->lse", inputs_all, weight_flat, preferred_element_type=jnp.float32)
        + bias_flat
    )
    qkv = qkv.astype(jnp.bfloat16)
    heads_major = qkv.reshape(length, seqs, 3, heads, HD).transpose(1, 2, 3, 0, 4)
    query = heads_major[:, 0]
    keyed = heads_major[:, 1]
    valued = heads_major[:, 2]
    mixed, logsum = lax.map(attend_forward, (query, keyed, valued, cluster_order))
    mixed_low = mixed.transpose(2, 0, 1, 3).reshape(length, seqs, local_width).astype(jnp.bfloat16)
    picked_tokens = mixed_low
    attended = lax.psum_scatter(
        jnp.einsum("lse,ed->lsd", picked_tokens, out_weight, preferred_element_type=jnp.float32),
        "tensor",
        scatter_dimension=0,
        tiled=True,
    )
    attended = attended + out_bias.astype(jnp.float32)
    resid_first = inputs.astype(jnp.float32) + attended
    first_normed, first_pull = jax.vjp(
        layer_norm, resid_first, first_gain.astype(jnp.float32), first_shift.astype(jnp.float32)
    )
    first_normed_full = lax.all_gather(
        first_normed.astype(jnp.bfloat16), "tensor", axis=0, tiled=True
    )
    upper_hidden = jnp.einsum(
        "zvn,nr->zvr", first_normed_full, first_layer_weight, preferred_element_type=jnp.float32
    )
    upper_hidden = upper_hidden + first_layer_bias.astype(jnp.float32)
    active_tokens, gelu_pull = jax.vjp(gelu_exact, upper_hidden)
    active_reduced = active_tokens.astype(jnp.bfloat16)
    picked_tokens = active_reduced
    lowered_rows = lax.psum_scatter(
        jnp.einsum(
            "ijg,gk->ijk", picked_tokens, second_layer_weight, preferred_element_type=jnp.float32
        ),
        "tensor",
        scatter_dimension=0,
        tiled=True,
    ) + second_layer_bias.astype(jnp.float32)
    result, second_pull = jax.vjp(
        layer_norm,
        first_normed + lowered_rows,
        second_gain.astype(jnp.float32),
        second_shift.astype(jnp.float32),
    )
    outputs = result.astype(jnp.bfloat16)
    token_ids = rank * shard + jnp.arange(shard, dtype=jnp.int32)
    hits = (masked_rows[:, :, None] == token_ids[None, None, :]).astype(jnp.bfloat16)
    dense_grad = jnp.einsum("smt,smd->tsd", hits, masked_grad, preferred_element_type=jnp.float32)
    d_second, grad_secondgain, grad_secondshift = second_pull(dense_grad)
    d_lowered = d_second.astype(jnp.bfloat16)
    grad_downbias = jnp.sum(d_lowered, axis=(0, 1), dtype=jnp.float32)
    lowered_gradient_full = lax.all_gather(d_lowered, "tensor", axis=0, tiled=True)
    grad_downweight = jnp.einsum(
        "zbr,zbv->rv", active_reduced, lowered_gradient_full, preferred_element_type=jnp.float32
    )
    d_active = jnp.einsum(
        "eah,jh->eaj",
        lowered_gradient_full,
        second_layer_weight,
        preferred_element_type=jnp.float32,
    )
    upper_gradient = gelu_pull(d_active)[0].astype(jnp.bfloat16)
    grad_upbias = jnp.sum(upper_gradient, axis=(0, 1), dtype=jnp.float32)
    grad_upweight = jnp.einsum(
        "gwp,gwm->pm", first_normed_full, upper_gradient, preferred_element_type=jnp.float32
    )
    picked_tokens = upper_gradient
    d_first = d_second + lax.psum_scatter(
        jnp.einsum(
            "qrh,ah->qra", picked_tokens, first_layer_weight, preferred_element_type=jnp.float32
        ),
        "tensor",
        scatter_dimension=0,
        tiled=True,
    )
    d_resid, grad_firstgain, grad_firstshift = first_pull(d_first)
    d_attended = d_resid.astype(jnp.bfloat16)
    grad_outbias = jnp.sum(d_attended, axis=(0, 1), dtype=jnp.float32)
    d_attended_all = lax.all_gather(d_attended, "tensor", axis=0, tiled=True)
    grad_outweight = jnp.einsum(
        "lse,lsd->ed", mixed_low, d_attended_all, preferred_element_type=jnp.float32
    )
    d_mixed = jnp.einsum(
        "lsd,ed->lse", d_attended_all, out_weight, preferred_element_type=jnp.float32
    ).astype(jnp.bfloat16)
    upstream = d_mixed.reshape(length, seqs, heads, HD).transpose(1, 2, 0, 3)
    d_heads = lax.map(attend_backward, (query, keyed, valued, upstream, cluster_order, logsum))
    d_qkv = d_heads.transpose(3, 0, 1, 2, 4).reshape(length, seqs, 3 * local_width)
    part_sums = jnp.sum(d_qkv, axis=(0, 1), dtype=jnp.float32).reshape(3, local_width)
    grad_qvbias = jnp.stack([part_sums[0], part_sums[2]])
    grad_qkvweight = jnp.einsum(
        "lsd,lse->de", inputs_all, d_qkv, preferred_element_type=jnp.float32
    ).reshape(width, 3, local_width)
    picked_tokens = d_qkv
    grad_inputs = d_resid + lax.psum_scatter(
        jnp.einsum(
            "lse,de->lsd", picked_tokens, weight_flat, preferred_element_type=jnp.float32
        ).astype(jnp.bfloat16),
        "tensor",
        scatter_dimension=0,
        tiled=True,
    ).astype(jnp.float32)
    grad_qkvweight, grad_qvbias, grad_outweight, grad_upweight, grad_upbias, grad_downweight = (
        lax.psum(
            (
                grad_qkvweight,
                grad_qvbias,
                grad_outweight,
                grad_upweight,
                grad_upbias,
                grad_downweight,
            ),
            "dp",
        )
    )
    (
        grad_outbias,
        grad_firstgain,
        grad_firstshift,
        grad_downbias,
        grad_secondgain,
        grad_secondshift,
    ) = lax.psum(
        (
            grad_outbias,
            grad_firstgain,
            grad_firstshift,
            grad_downbias,
            grad_secondgain,
            grad_secondshift,
        ),
        ("dp", "tensor"),
    )
    return (
        outputs,
        grad_inputs,
        grad_qkvweight,
        grad_qvbias,
        grad_outweight,
        grad_outbias,
        grad_firstgain,
        grad_firstshift,
        grad_upweight,
        grad_upbias,
        grad_downweight,
        grad_downbias,
        grad_secondgain,
        grad_secondshift,
    )


def solution(mesh):
    placed = (
        P("tensor", "dp", None),
        P(None, None, "tensor"),
        P(None, "tensor"),
        P("tensor", None),
        P(),
        P(),
        P(),
        P(None, "tensor"),
        P("tensor"),
        P("tensor", None),
        P(),
        P(),
        P(),
        P("dp", "tensor", None),
        P("dp", None),
        P("dp", None, None),
    )
    return jax.shard_map(
        shards,
        mesh=mesh,
        in_specs=placed,
        out_specs=(
            P("tensor", "dp", None),
            P("tensor", "dp", None),
            P(None, None, "tensor"),
            P(None, "tensor"),
            P("tensor", None),
            P(),
            P(),
            P(),
            P(None, "tensor"),
            P("tensor"),
            P("tensor", None),
            P(),
            P(),
            P(),
        ),
        check_vma=False,
    )
```

profile of v0, /device:TPU:9, one launch (start us, length us, event | category | flops | bytes accessed | tf_op | source)
XLA Modules:
  0.0 1265.7 jit_solution(15747524355812453695)
XLA Ops:
  10.2 62.2 %all-gather.5.cloned.1.call-done = bf16[1024,2,768]{2,0,1:T(8,128)(2,1)} async-done(((bf16[256,2,768]{2,0,1:T(8,128)(2,1)}), bf16[1024,2,768]{2,0,1:T(8,128)(2,1)}) %all-gather.5.cloned.1.call-update) | async-done | bytes 3145744 | tf_op jit(solution)/shard_map/all_gather | solution.py:125
  85.2 139.1 %while.22 = (s32[]{:T(128)}, bf16[2,3,1024,64]{2,3,1,0:T(8,128)(2,1)}, f32[2,3,8,128,1]{3,2,1,4,0:T(8,128)}, s32[2,3,1024]{2,1,0:T(4,128)}, bf16[2,3,1024,64]{3,...) while((s32[]{:T(128)}, ...), condition=%wide.region_4.6_spmd, body=%wide.region_0.5_spmd.sunk | while | flops 104100864 | bytes 21075200 | solution.py:135
  88.0 16.4 %gather_fusion = bf16[3072,64]{1,0:T(8,128)(2,1)S(1)} fusion(bf16[3,1024,64]{2,1,0:T(8,128)(2,1)S(1)} %get-tuple-element.388, s32[3072]{0:T(1024)S(1)} %reshape.517), kind=kCustom, calls=%fused_computation.2.clone.clone.1 | custom fusion | bytes 811008 | tf_op jit(solution)/shard_map/while/body/eval_jaxpr/vmap(jit(_take))/gather | solution.py:26
  105.4 16.4 %gather_fusion.1 = bf16[3072,64]{1,0:T(8,128)(2,1)S(1)} fusion(bf16[3,1024,64]{2,1,0:T(8,128)(2,1)S(1)} %get-tuple-element.390, s32[3072]{0:T(1024)S(1)} %reshape.517), kind=kCustom, calls=%fused_computation.1.clone.clone.1 | custom fusion | bytes 811008 | tf_op jit(solution)/shard_map/while/body/eval_jaxpr/vmap(jit(_take))/gather | solution.py:26
  123.3 16.4 %gather_fusion.2 = bf16[3072,64]{1,0:T(8,128)(2,1)S(1)} fusion(bf16[3,1024,64]{2,1,0:T(8,128)(2,1)S(1)} %dynamic-slice_bitcast_fusion.14, s32[3072]{0:T(1024)S(1)} %reshape.517), kind=kCustom, calls=%fused_computation.clone.clone.1 | custom fusion | bytes 811008 | tf_op jit(solution)/shard_map/while/body/eval_jaxpr/vmap(jit(_take))/gather | solution.py:26
  157.5 16.4 %gather_fusion = bf16[3072,64]{1,0:T(8,128)(2,1)S(1)} fusion(bf16[3,1024,64]{2,1,0:T(8,128)(2,1)S(1)} %get-tuple-element.388, s32[3072]{0:T(1024)S(1)} %reshape.517), kind=kCustom, calls=%fused_computation.2.clone.clone.1 | custom fusion | bytes 811008 | tf_op jit(solution)/shard_map/while/body/eval_jaxpr/vmap(jit(_take))/gather | solution.py:26
  175.0 16.4 %gather_fusion.1 = bf16[3072,64]{1,0:T(8,128)(2,1)S(1)} fusion(bf16[3,1024,64]{2,1,0:T(8,128)(2,1)S(1)} %get-tuple-element.390, s32[3072]{0:T(1024)S(1)} %reshape.517), kind=kCustom, calls=%fused_computation.1.clone.clone.1 | custom fusion | bytes 811008 | tf_op jit(solution)/shard_map/while/body/eval_jaxpr/vmap(jit(_take))/gather | solution.py:26
  192.9 16.4 %gather_fusion.2 = bf16[3072,64]{1,0:T(8,128)(2,1)S(1)} fusion(bf16[3,1024,64]{2,1,0:T(8,128)(2,1)S(1)} %dynamic-slice_bitcast_fusion.14, s32[3072]{0:T(1024)S(1)} %reshape.517), kind=kCustom, calls=%fused_computation.clone.clone.1 | custom fusion | bytes 811008 | tf_op jit(solution)/shard_map/while/body/eval_jaxpr/vmap(jit(_take))/gather | solution.py:26
  229.9 111.4 %reduce-scatter.5.cloned.1.call-done = f32[256,2,768]{2,0,1:T(8,128)} async-done(((f32[1024,2,768]{2,0,1:T(8,128)}), f32[256,2,768]{2,0,1:T(8,128)}) %reduce-scatter.5.cloned.1.call-update) | async-done | bytes 1572880 | tf_op jit(solution)/shard_map/reduce_scatter | solution.py:138
  344.8 61.4 %all-gather.7.cloned.1.call-done = bf16[1024,2,768]{2,0,1:T(8,128)(2,1)} async-done(((bf16[256,2,768]{2,0,1:T(8,128)(2,1)}), bf16[1024,2,768]{2,0,1:T(8,128)(2,1)}) %all-gather.7.cloned.1.call-update) | async-done | bytes 3145744 | tf_op jit(solution)/shard_map/all_gather | solution.py:149
  412.6 15.6 %multiply_convert_fusion.1 = (bf16[1024,2,768]{2,0,1:T(8,128)(2,1)S(1)}, f32[1024,2,768]{2,0,1:T(8,128)}) fusion(f32[1024,2,768]{2,0,1:T(8,128)S(1)} %get-tuple-element.278, f32[768]{0:T(1024)S(1)} %convert_element_type.119, u8[1024,768]{1,0:T(8,128)(4,1)S(1)} %get-tuple-element.186, u8[1024,768]{1,0:T(8,128)(4,1)S(1)} %get-tuple-element.185), kind=kLoop, calls=%fused_computation.96 | loop fusion | flops 111673344 | bytes 17304576 | tf_op jit(solution)/shard_map/convert_element_type | solution.py:157
  435.2 111.4 %reduce-scatter.7.cloned.1.call-done = f32[256,2,768]{2,0,1:T(8,128)} async-done(((f32[1024,2,768]{2,0,1:T(8,128)}), f32[256,2,768]{2,0,1:T(8,128)}) %reduce-scatter.7.cloned.1.call-update) | async-done | bytes 1572880 | tf_op jit(solution)/shard_map/reduce_scatter | solution.py:159
  555.8 61.2 %all-gather.9.cloned.1.call-done = bf16[1024,2,768]{2,0,1:T(8,128)(2,1)} async-done(((bf16[256,2,768]{2,0,1:T(8,128)(2,1)}), bf16[1024,2,768]{2,0,1:T(8,128)(2,1)}) %all-gather.9.cloned.1.call-update) | async-done | bytes 3145744 | tf_op jit(solution)/shard_map/all_gather | solution.py:180
  617.0 11.1 convert_reduce_fusion
  634.3 112.0 %reduce-scatter.9.cloned.1.call-done = f32[256,2,768]{2,0,1:T(8,128)} async-done(((f32[1024,2,768]{2,0,1:T(8,128)}), f32[256,2,768]{2,0,1:T(8,128)}) %reduce-scatter.9.cloned.1.call-update) | async-done | bytes 1572880 | tf_op jit(solution)/shard_map/reduce_scatter | solution.py:196
  753.2 61.6 %all-gather.11.cloned.1.call-done = bf16[1024,2,768]{2,0,1:T(8,128)(2,1)} async-done(((bf16[256,2,768]{2,0,1:T(8,128)(2,1)}), bf16[1024,2,768]{2,0,1:T(8,128)(2,1)}) %all-gather.11.cloned.1.call-update) | async-done | bytes 3145744 | tf_op jit(solution)/shard_map/all_gather | solution.py:207
  818.7 245.0 %while.23 = (s32[]{:T(128)}, bf16[2,3,3,1024,64]{3,4,2,1,0:T(8,128)(2,1)}, s32[2,3,1024]{2,1,0:T(4,128)}, bf16[2,3,1024,64]{3,2,1,0:T(8,128)(2,1)}, bf16[2,3,102...) while((s32[]{:T(128)}, ...), condition=%wide.region_21.23_spmd, body=%wide.region_16.22_spmd.sunk | while | flops 257848320 | bytes 58665428 | solution.py:215
  820.9 16.4 %gather_fusion.3 = bf16[3072,64]{1,0:T(8,128)(2,1)S(1)} fusion(bf16[3,1024,64]{2,1,0:T(8,128)(2,1)S(1)} %get-tuple-element.405, s32[3072]{0:T(1024)S(1)} %reshape.533), kind=kCustom, calls=%fused_computation.6.clone.clone.1 | custom fusion | bytes 811008 | tf_op jit(solution)/shard_map/while/body/eval_jaxpr/vmap(jit(_take))/gather | solution.py:26
  839.8 16.4 %gather_fusion.4 = bf16[3072,64]{1,0:T(8,128)(2,1)S(1)} fusion(bf16[3,1024,64]{2,1,0:T(8,128)(2,1)S(1)} %get-tuple-element.407, s32[3072]{0:T(1024)S(1)} %reshape.533), kind=kCustom, calls=%fused_computation.4.clone.clone.1 | custom fusion | bytes 811008 | tf_op jit(solution)/shard_map/while/body/eval_jaxpr/vmap(jit(_take))/gather | solution.py:26
  857.3 16.4 %gather_fusion.5 = bf16[3072,64]{1,0:T(8,128)(2,1)S(1)} fusion(bf16[3,1024,64]{2,1,0:T(8,128)(2,1)S(1)} %get-tuple-element.408, s32[3072]{0:T(1024)S(1)} %reshape.533), kind=kCustom, calls=%fused_computation.5.clone.clone.1 | custom fusion | bytes 811008 | tf_op jit(solution)/shard_map/while/body/eval_jaxpr/vmap(jit(_take))/gather | solution.py:26
  874.0 16.4 %gather_fusion.6 = bf16[3072,64]{1,0:T(8,128)(2,1)S(1)} fusion(bf16[3,1024,64]{2,1,0:T(8,128)(2,1)S(1)} %get-tuple-element.409, s32[3072]{0:T(1024)S(1)} %reshape.533), kind=kCustom, calls=%fused_computation.3.clone.clone.1 | custom fusion | bytes 811008 | tf_op jit(solution)/shard_map/while/body/eval_jaxpr/vmap(jit(_take))/gather | solution.py:26
  897.5 9.6 scatter_custom_fusion.23
  913.9 9.6 scatter_custom_fusion.22
  943.2 16.4 %gather_fusion.3 = bf16[3072,64]{1,0:T(8,128)(2,1)S(1)} fusion(bf16[3,1024,64]{2,1,0:T(8,128)(2,1)S(1)} %get-tuple-element.405, s32[3072]{0:T(1024)S(1)} %reshape.533), kind=kCustom, calls=%fused_computation.6.clone.clone.1 | custom fusion | bytes 811008 | tf_op jit(solution)/shard_map/while/body/eval_jaxpr/vmap(jit(_take))/gather | solution.py:26
  962.1 16.4 %gather_fusion.4 = bf16[3072,64]{1,0:T(8,128)(2,1)S(1)} fusion(bf16[3,1024,64]{2,1,0:T(8,128)(2,1)S(1)} %get-tuple-element.407, s32[3072]{0:T(1024)S(1)} %reshape.533), kind=kCustom, calls=%fused_computation.4.clone.clone.1 | custom fusion | bytes 811008 | tf_op jit(solution)/shard_map/while/body/eval_jaxpr/vmap(jit(_take))/gather | solution.py:26
  979.6 16.4 %gather_fusion.5 = bf16[3072,64]{1,0:T(8,128)(2,1)S(1)} fusion(bf16[3,1024,64]{2,1,0:T(8,128)(2,1)S(1)} %get-tuple-element.408, s32[3072]{0:T(1024)S(1)} %reshape.533), kind=kCustom, calls=%fused_computation.5.clone.clone.1 | custom fusion | bytes 811008 | tf_op jit(solution)/shard_map/while/body/eval_jaxpr/vmap(jit(_take))/gather | solution.py:26
  996.3 16.4 %gather_fusion.6 = bf16[3072,64]{1,0:T(8,128)(2,1)S(1)} fusion(bf16[3,1024,64]{2,1,0:T(8,128)(2,1)S(1)} %get-tuple-element.409, s32[3072]{0:T(1024)S(1)} %reshape.533), kind=kCustom, calls=%fused_computation.3.clone.clone.1 | custom fusion | bytes 811008 | tf_op jit(solution)/shard_map/while/body/eval_jaxpr/vmap(jit(_take))/gather | solution.py:26
  1019.8 9.6 scatter_custom_fusion.23
  1036.2 9.6 scatter_custom_fusion.22
  1090.5 45.8 %all-reduce = (f32[768]{0:T(1024)}, f32[768]{0:T(1024)}, f32[768]{0:T(1024)}, f32[768]{0:T(1024)}, f32[768]{0:T(1024)}, /*index=5*/f32[768]{0:T(1024)}) all-reduce(f32[768]{0:T(1024)S(1)} %copy-done.35, f32[768]{0:T(1024)S(1)} %copy-done.36, f32[768]{0:T(1024)S(1)} %copy-done.37, ...), channel_id=1, replica_groups=mesh['dp'=8,'tensor'=4] {'dp','tensor'}, use_global_device_ids=true, to_apply=%region_28.30 | all-reduce | flops 4608 | bytes 36864 | tf_op jit(solution)/shard_map/psum | solution.py:251
  1138.5 13.5 %all-reduce.1 = (f32[2,192]{1,0:T(2,128)}, f32[768]{0:T(1024)}) all-reduce(f32[2,192]{1,0:T(2,128)S(1)} %pad_maximum_fusion.2, f32[768]{0:T(1024)S(1)} %copy-done.38), channel_id=1, replica_groups=mesh['dp'=8,'tensor'=4] {'dp'}, use_global_device_ids=true, to_apply=%region_25.27 | all-reduce | flops 1152 | bytes 9216 | tf_op jit(solution)/shard_map/psum | solution.py:232
  1155.7 95.3 %all-reduce.5.cloned.1.call-done = (f32[768,3,192]{0,2,1:T(8,128)}, f32[192,768]{1,0:T(8,128)}, f32[768,768]{1,0:T(8,128)}, f32[768,768]{1,0:T(8,128)}) async-done(((f32[768,3,192]{0,2,1:T(8,128)}, f32[192,768]{1,0:T(8,128)}, f32[768,768]{1,0:T(8,128)}, f32[768,768]{1,0:T(8,128)}), (f32[768,3,192]{0,2,1:T(8,128)}, f32[192,768]{1,0:T(8,128)}, f32[768,768]{1,0:T(8,128)}, ...) | async-done | bytes 7077904 | tf_op jit(solution)/shard_map/psum | solution.py:232
  (321 shorter events, 219.1 us)
Async XLA Ops:
  7.2 399.0 %copy-start = (bf16[768,768]{1,0:T(8,128)(2,1)S(1)}, bf16[768,768]{1,0:T(8,128)(2,1)}, u32[]{:S(2)}) copy-start(bf16[768,768]{1,0:T(8,128)(2,1)} %param.29) | copy-start | bytes 3538948
  7.2 3.0 copy-start.39
  7.2 65.2 %all-gather.5.cloned.1.call-start = ((), (), s32[]{:S(2)}) async-start(), calls=%async_computation.4 | async-start | bytes 3932160 | tf_op jit(solution)/shard_map/all_gather | solution.py:125
  9.5 331.8 %reduce-scatter.5.cloned.1.call-start = ((), (), s32[]{:S(2)}) async-start(), calls=%async_computation.5 | async-start | bytes 7864320 | tf_op jit(solution)/shard_map/reduce_scatter | solution.py:138
  123.3 17.5 %copy-start.6 = (bf16[3,1024,64]{1,2,0:T(8,128)(2,1)S(1)}, bf16[3,1024,64]{1,2,0:T(8,128)(2,1)}, u32[]{:S(2)}) copy-start(bf16[3,1024,64]{1,2,0:T(8,128)(2,1)} %copy.244) | copy-start | bytes 1179652 | tf_op jit(solution)/shard_map/while
  192.9 17.5 %copy-start.6 = (bf16[3,1024,64]{1,2,0:T(8,128)(2,1)S(1)}, bf16[3,1024,64]{1,2,0:T(8,128)(2,1)}, u32[]{:S(2)}) copy-start(bf16[3,1024,64]{1,2,0:T(8,128)(2,1)} %copy.244) | copy-start | bytes 1179652 | tf_op jit(solution)/shard_map/while
  229.2 112.1 %copy-start.18 = (bf16[256,2,768]{2,1,0:T(2,128)(2,1)S(1)}, bf16[256,2,768]{2,1,0:T(2,128)(2,1)}, u32[]{:S(2)}) copy-start(bf16[256,2,768]{2,1,0:T(2,128)(2,1)} %param.22) | copy-start | bytes 2359300
  229.2 177.0 %all-gather.7.cloned.1.call-start = ((), (), s32[]{:S(2)}) async-start(), calls=%async_computation.6 | async-start | bytes 3932160 | tf_op jit(solution)/shard_map/all_gather | solution.py:149
  344.5 202.0 %reduce-scatter.7.cloned.1.call-start = ((), (), s32[]{:S(2)}) async-start(), calls=%async_computation.7 | async-start | bytes 7864320 | tf_op jit(solution)/shard_map/reduce_scatter | solution.py:159
  412.6 15.6 %copy-start.12 = (f32[1024,2,768]{2,0,1:T(8,128)}, f32[1024,2,768]{2,0,1:T(8,128)S(1)}, u32[]{:S(2)}) copy-start(f32[1024,2,768]{2,0,1:T(8,128)S(1)} %get-tuple-element.278) | copy-start | bytes 18874372
  412.6 17.4 %copy-start.50 = (bf16[768,768]{1,0:T(8,128)(2,1)S(1)}, bf16[768,768]{1,0:T(8,128)(2,1)}, u32[]{:S(2)}) copy-start(bf16[768,768]{1,0:T(8,128)(2,1)} %param.31) | copy-start | bytes 3538948
  434.5 182.5 %all-gather.9.cloned.1.call-start = ((), (), s32[]{:S(2)}) async-start(), calls=%async_computation.8 | async-start | bytes 3932160 | tf_op jit(solution)/shard_map/all_gather | solution.py:180
  555.3 191.1 %reduce-scatter.9.cloned.1.call-start = ((), (), s32[]{:S(2)}) async-start(), calls=%async_computation.9 | async-start | bytes 7864320 | tf_op jit(solution)/shard_map/reduce_scatter | solution.py:196
  634.3 180.5 %all-gather.11.cloned.1.call-start = ((), (), s32[]{:S(2)}) async-start(), calls=%async_computation.10 | async-start | bytes 3932160 | tf_op jit(solution)/shard_map/all_gather | solution.py:207
  751.4 63.4 %copy-start.25 = (bf16[192,768]{1,0:T(8,128)(2,1)S(1)}, bf16[192,768]{1,0:T(8,128)(2,1)}, u32[]{:S(2)}) copy-start(bf16[192,768]{1,0:T(8,128)(2,1)} %param.25) | copy-start | bytes 884740
  753.1 398.9 %reduce-scatter.11.cloned.1.call-start = ((), (), s32[]{:S(2)}) async-start(), calls=%async_computation.11 | async-start | bytes 3932160 | tf_op jit(solution)/shard_map/reduce_scatter | solution.py:223
  874.0 17.5 %copy-start.4 = (bf16[3,1024,64]{1,2,0:T(8,128)(2,1)S(1)}, bf16[3,1024,64]{1,2,0:T(8,128)(2,1)}, u32[]{:S(2)}) copy-start(bf16[3,1024,64]{1,2,0:T(8,128)(2,1)} %copy.255) | copy-start | bytes 1179652 | tf_op jit(solution)/shard_map/while
  874.0 17.5 %copy-start.5 = (bf16[3,1024,64]{1,2,0:T(8,128)(2,1)S(1)}, bf16[3,1024,64]{1,2,0:T(8,128)(2,1)}, u32[]{:S(2)}) copy-start(bf16[3,1024,64]{1,2,0:T(8,128)(2,1)} %copy.256) | copy-start | bytes 1179652 | tf_op jit(solution)/shard_map/while
  996.2 17.5 %copy-start.4 = (bf16[3,1024,64]{1,2,0:T(8,128)(2,1)S(1)}, bf16[3,1024,64]{1,2,0:T(8,128)(2,1)}, u32[]{:S(2)}) copy-start(bf16[3,1024,64]{1,2,0:T(8,128)(2,1)} %copy.255) | copy-start | bytes 1179652 | tf_op jit(solution)/shard_map/while
  996.3 17.5 %copy-start.5 = (bf16[3,1024,64]{1,2,0:T(8,128)(2,1)S(1)}, bf16[3,1024,64]{1,2,0:T(8,128)(2,1)}, u32[]{:S(2)}) copy-start(bf16[3,1024,64]{1,2,0:T(8,128)(2,1)} %copy.256) | copy-start | bytes 1179652 | tf_op jit(solution)/shard_map/while
  1069.9 181.1 %all-reduce.5.cloned.1.call-start = ((), (), s32[]{:S(2)}) async-start(), calls=%async_computation.12 | async-start | bytes 14155776 | tf_op jit(solution)/shard_map/psum | solution.py:232
  1070.0 7.1 copy-start.49
  1070.0 7.1 copy-start.54
  1077.1 4.2 copy-start.17
  1077.1 4.2 copy-start.19
  1077.1 5.8 copy-start.48
  1090.4 48.1 %copy-start.38 = (f32[768]{0:T(1024)S(1)}, f32[768]{0:T(1024)}, u32[]{:S(2)}) copy-start(f32[768]{0:T(1024)} %get-tuple-element.280) | copy-start | bytes 9220
  1090.4 61.6 %copy-start.10 = (f32[256,2,768]{2,0,1:T(8,128)S(1)}, f32[256,2,768]{2,0,1:T(8,128)}, u32[]{:S(2)}) copy-start(f32[256,2,768]{2,0,1:T(8,128)} %copy-done.9) | copy-start | bytes 4718596
  1090.4 61.6 %copy-start.33 = (f32[256,2]{0,1:T(2,128)S(1)}, f32[256,2]{0,1:T(2,128)}, u32[]{:S(2)}) copy-start(f32[256,2]{0,1:T(2,128)} %copy-done.32) | copy-start | bytes 6148
  1251.0 3.0 copy-start.24
  1251.0 3.8 copy-start.22
  1254.8 3.9 copy-start.1
  (45 other events, 74.8 us)
Sparse Core Ops, SparseCore 0:
  10.2 62.2 all-gather.4
  229.4 111.8 reduce-scatter.4
  344.6 61.5 all-gather.6
  434.6 111.9 reduce-scatter.6
  555.4 61.4 all-gather.8
  634.4 111.9 reduce-scatter.8
  753.2 61.4 all-gather.10
  1070.0 61.9 reduce-scatter.10
  1136.9 114.0 all-reduce.4
where the time goes:
time: 1280 us; the launch traced here: 1270 us
  waiting for transfers between devices  677 us (53%)
  local copies, waits for them, and re-layouts  379 us (30%)
  matrix products  77 us (6%)
  blocking collectives  59.3 us (5%)
  other arithmetic  56.9 us (4%)
  between operations  14.7 us (1%)
    gather x32, local copies, waits for them, and re-layouts, sort_heads(): jnp.take(block, picks, axis=0)  238 us
    reduce_scatter x1, waiting for transfers between devices, shards(): lax.psum_scatter(jnp.einsum('qrh,ah->qra', picked_tokens, first_layer_wei...  112 us
    reduce_scatter x1, waiting for transfers between devices, shards(): lax.psum_scatter(jnp.einsum('ijg,gk->ijk', picked_tokens, second_layer_we...  111 us
    reduce_scatter x1, waiting for transfers between devices, shards(): lax.psum_scatter(jnp.einsum('lse,ed->lsd', picked_tokens, out_weight, pre...  111 us
    psum x1, waiting for transfers between devices, shards(): lax.psum((grad_qkvweight, grad_qvbias, grad_outweight, grad_upweight, gra...  95.3 us
    while x68, local copies, waits for them, and re-layouts  78.6 us
    all_gather x1, waiting for transfers between devices, shards(): inputs_all = lax.all_gather(inputs, 'tensor', axis=0, tiled=True)  62.2 us
    all_gather x1, waiting for transfers between devices, shards(): d_attended_all = lax.all_gather(d_attended, 'tensor', axis=0, tiled=True)  61.6 us
  transfers between devices with their start and end apart: 9, of which 8 were waited for; matrix products, arithmetic and copies ran while one was open for 2% of the time, Pallas kernels for 0%

commit v1 on v0

v1 whole, which is shorter than its diff:
```python
import math

import jax
import jax.numpy as jnp
from jax import lax
from jax.experimental import pallas as pl
from jax.experimental.pallas import tpu as pltpu
from jax.sharding import PartitionSpec as P

HD = 64
C = 128
NORM_EPS = 1e-05
BF = jnp.bfloat16
F32 = jnp.float32
MESH = pl.DeviceIdType.MESH
RSQRT2 = 1.0 / math.sqrt(2.0)
RSQRT2PI = 1.0 / math.sqrt(2.0 * math.pi)

NN = (((1,), (0,)), ((), ()))
NT = (((1,), (1,)), ((), ()))
TN = (((0,), (0,)), ((), ()))


def mm(a, b, dims=NN):
    return lax.dot_general(a, b, dims, preferred_element_type=F32)


def kernel(
    x_in, ord_in, wa_in, wb_in, wc_in, bias_in, par, mr_in, mg_in,
    o1, o2, res, vout,
    xall, ordv, wg, bias, mr, mg, wm, wo, qkv, oc, sq, skv, pr, ms, mix,
    snd, rcv, op, fst, n1, rs1, flow, act, dg, dl, da, dm, g, st1, st2, st3,
    rb, tok, gtok, vb, vr,
    x_s, x_r, x_l, cx_s, cx_r, o_s, o_r, o_l, b_s, b_r, b_l, m_s, m_r, m_l,
    wz_s, wz_s2, wz_r, wx_s, wx_r, w_l, pe_s, pe_r, t_s, t_r, t_l, v_s, v_r,
    g1_s, g1_r, g2_s, g2_r, g3_s, g3_r, ag_s, ag_r, ag_l, ce_s, ce_r,
):
    w_in = (wa_in, wb_in, wc_in)
    d = lax.axis_index("dp")
    z = lax.axis_index("tensor")
    c = lax.rem(d, 2)
    base = d - c
    sib = base + 1 - c
    px = lax.rem(lax.div(d, 2), 2)
    py = lax.rem(lax.div(d, 4), 2)
    xn = d + 2 - 4 * px
    yn = d + 4 - 8 * py
    zc = lax.div(z, 2)
    zj = lax.rem(z, 2)
    up = 1 - 2 * c
    zz = 3 * c + z * up
    prim = zc == c

    def rc(src, dst, ss, rs, dev):
        return pltpu.make_async_remote_copy(
            src_ref=src, dst_ref=dst, send_sem=ss, recv_sem=rs,
            device_id=dev, device_id_type=MESH,
        )

    def wait_send(src, ss):
        rc(src, src, ss, ss, (sib, z)).wait_send()

    def wait_recv(dst, rs):
        rc(dst, dst, rs, rs, (sib, z)).wait_recv()

    def lc(src, dst, sem):
        return pltpu.make_async_copy(src, dst, sem)

    bar = pltpu.get_barrier_semaphore()
    for k in range(1, 8):
        oc_, oz = k % 2, k // 2
        dev = (base + lax.rem(c + oc_, 2), lax.rem(z + oz, 4))
        pl.semaphore_signal(bar, inc=1, device_id=dev, device_id_type=MESH)
    for dev in ((xn, z), (yn, z)):
        pl.semaphore_signal(bar, inc=1, device_id=dev, device_id_type=MESH)
    pl.semaphore_wait(bar, 9)

    def pp(r):
        return (px, py) if r == 0 else (py, px)

    def nbs(r):
        return ((xn, z), (yn, z)) if r == 0 else ((yn, z), (xn, z))

    def blk(r, p1, p2):
        return pl.ds(pl.multiple_of(384 * r + 96 * (2 * p1 + p2), 32), 96)

    def uof(v):
        return c + v * up

    def w_start(a):
        for v in range(2):
            for r in range(2):
                p1, p2 = pp(r)
                rows = blk(r, p1, p2)
                src = w_in[a].at[rows]
                dst = wg.at[a, uof(v), rows]

                @pl.when(zz == v)
                def _(src=src, dst=dst, v=v, r=r):
                    rc(src, dst, wz_s.at[a, v, r], wz_r.at[a, v, r], (d, z + up)).start()
                    if v == 1:
                        rc(src, dst, wz_s2.at[a, r], wz_r.at[a, v, r], (d, z - up)).start()

    def w_local(a):
        for v in range(2):

            @pl.when(zz == v)
            def _(v=v):
                lc(w_in[a], wg.at[a, uof(v)], w_l.at[a]).start()

    def w_fwd(a):
        for v in range(2):
            for r in range(2):
                p1, p2 = pp(r)
                ref = wg.at[a, uof(v), blk(r, p1, p2)]
                n1_, n2_ = nbs(r)

                @pl.when(zz != v)
                def _(ref=ref, v=v, r=r, n1_=n1_, n2_=n2_):
                    wait_recv(ref, wz_r.at[a, v, r])
                    rc(ref, ref, wx_s.at[a, v, r, 0], wx_r.at[a, v, r, 0], n1_).start()
                    rc(ref, ref, wx_s.at[a, v, r, 1], wx_r.at[a, v, r, 1], n2_).start()

                fw = ((zz == 1) | (zz == 2)) if v == 0 else (zz == 2)

                @pl.when(fw)
                def _(ref=ref, v=v, r=r):
                    rc(ref, ref, wz_s.at[a, v, r], wz_r.at[a, v, r], (d, z + up)).start()

    def w_fwd2(a):
        for v in range(2):
            for r in range(2):
                p1, p2 = pp(r)
                ref = wg.at[a, uof(v), blk(r, 1 - p1, p2)]
                n1_, n2_ = nbs(r)

                @pl.when(zz != v)
                def _(ref=ref, v=v, r=r, n2_=n2_):
                    wait_recv(ref, wx_r.at[a, v, r, 0])
                    rc(ref, ref, wx_s.at[a, v, r, 2], wx_r.at[a, v, r, 2], n2_).start()

    def w_done(a):
        for v in range(2):
            for r in range(2):
                p1, p2 = pp(r)

                @pl.when(zz != v)
                def _(v=v, r=r, p1=p1, p2=p2):
                    wait_recv(wg.at[a, uof(v), blk(r, p1, 1 - p2)], wx_r.at[a, v, r, 1])
                    wait_recv(wg.at[a, uof(v), blk(r, 1 - p1, 1 - p2)], wx_r.at[a, v, r, 2])

            @pl.when(zz == v)
            def _(v=v):
                lc(w_in[a], wg.at[a, uof(v)], w_l.at[a]).wait()

    def w_end(a):
        for v in range(2):
            for r in range(2):
                p1, p2 = pp(r)
                rows = blk(r, p1, p2)
                ref = wg.at[a, uof(v), rows]
                sent = (zz <= 2) if v == 0 else ((zz == 1) | (zz == 2))

                @pl.when(sent)
                def _(ref=ref, v=v, r=r):
                    wait_send(ref, wz_s.at[a, v, r])

                if v == 1:

                    @pl.when(zz == 1)
                    def _(ref=ref, r=r):
                        wait_send(ref, wz_s2.at[a, r])

                @pl.when(zz != v)
                def _(ref=ref, v=v, r=r):
                    for k in range(3):
                        wait_send(ref, wx_s.at[a, v, r, k])

    for j in range(2):
        dev = (base + zc, 2 * c + j)
        self_ = (zc == c) & (z == 2 * c + j)

        @pl.when(self_)
        def _(j=j):
            lc(ord_in.at[j], ordv.at[zj], o_l).start()

        @pl.when(jnp.logical_not(self_))
        def _(j=j, dev=dev):
            rc(ord_in.at[j], ordv.at[zj], o_s.at[j], o_r.at[zj], dev).start()

    @pl.when(prim)
    def _():
        for k in range(1, 4):
            dev = (d, lax.rem(z + k, 4))
            rc(bias_in, bias.at[zj], b_s.at[k - 1], b_r.at[zj], dev).start()
        lc(bias_in, bias.at[zj], b_l).start()
        lc(mr_in.at[zj], mr, m_l.at[0]).start()
        lc(mg_in.at[zj], mg, m_l.at[1]).start()
        rc(mr_in.at[zj], mr, m_s.at[0], m_r.at[0], (sib, z)).start()
        rc(mg_in.at[zj], mg, m_s.at[1], m_r.at[1], (sib, z)).start()

    w_start(0)
    w_local(0)

    for j in range(2):
        for h in range(2):
            zt = 2 * c + j
            rows = pl.ds(128 * h, 128)
            self_ = (c == h) & (z == zt)
            src = x_in.at[j, rows]
            dst = xall.at[z, rows]

            @pl.when(self_)
            def _(src=src, dst=dst):
                lc(src, dst, x_l).start()

            @pl.when(jnp.logical_not(self_))
            def _(src=src, dst=dst, j=j, h=h, zt=zt):
                rc(src, dst, x_s.at[j, h], x_r.at[z], (base + h, zt)).start()

    w_local(1)
    w_local(2)
    w_fwd(0)
    w_fwd2(0)
    w_start(1)
    w_start(2)
    crows = pl.ds(pl.multiple_of(128 * c, 128), 128)
    srows = pl.ds(pl.multiple_of(128 * (1 - c), 128), 128)
    for k in range(4):
        ref = xall.at[k, crows]
        loc = prim & (z == k)

        @pl.when(loc)
        def _(ref=ref):
            lc(ref, ref, x_l).wait()

        @pl.when(jnp.logical_not(loc))
        def _(ref=ref, k=k):
            wait_recv(ref, x_r.at[k])

        rc(ref, ref, cx_s.at[k], cx_r.at[k], (sib, z)).start()
    for k in range(4):
        wait_recv(xall.at[k, srows], cx_r.at[k])

    for u in range(2):
        loc = prim & (zj == u)

        @pl.when(loc)
        def _(u=u):
            lc(ord_in.at[0], ordv.at[u], o_l).wait()
            lc(bias_in, bias.at[u], b_l).wait()

        @pl.when(jnp.logical_not(loc))
        def _(u=u):
            wait_recv(ordv.at[u], o_r.at[u])
            wait_recv(bias.at[u], b_r.at[u])

    @pl.when(prim)
    def _():
        lc(mr_in.at[0], mr, m_l.at[0]).wait()
        lc(mg_in.at[0], mg, m_l.at[1]).wait()

    @pl.when(jnp.logical_not(prim))
    def _():
        wait_recv(mr, m_r.at[0])
        wait_recv(mg, m_r.at[1])

    w_done(0)

    lane = lax.broadcasted_iota(jnp.int32, (128, 128), 1)
    sub = lax.broadcasted_iota(jnp.int32, (128, 1024), 0)
    low = lane < 64
    lowb = lax.broadcasted_iota(jnp.int32, (768, 128), 1) < 64

    def pick(m, a, b):
        return jnp.where(m, a.astype(F32), b.astype(F32)).astype(BF)

    wm[:, 0:128] = wg[0, 0, :, 384:512]
    wm[:, 128:256] = pick(lowb, wg[0, 0, :, 640:768], wg[0, 1, :, 640:768])
    wm[:, 256:384] = wg[0, 1, :, 384:512]
    wo[:, 0:128] = wg[0, 0, :, 512:640]
    wo[:, 128:256] = pick(lowb, wg[0, 1, :, 640:768], wg[0, 0, :, 640:768])
    wo[:, 256:384] = wg[0, 1, :, 512:640]
    low1 = lax.broadcasted_iota(jnp.int32, (1, 128), 1) < 64

    def wq(i):
        if i == 1:
            return wm[...]
        return wg[0, i // 2, :, 0:384]

    def bq(i):
        if i == 1:
            return jnp.concatenate(
                [
                    bias[0, 0:1, 384:512],
                    jnp.where(low1, bias[0, 0:1, 640:768], bias[1, 0:1, 640:768]),
                    bias[1, 0:1, 384:512],
                ],
                axis=1,
            )
        return bias[i // 2, 0:1, 0:384]

    def rows_of(m, n):
        return pl.ds(pl.multiple_of(m * n, n), n)

    for i in range(3):
        wv = wq(i)
        bv = bq(i)

        def body(k, _, i=i, wv=wv, bv=bv):
            qkv[i, rows_of(k, 256), :] = (mm(xall[k], wv) + bv).astype(BF)
            return 0

        lax.fori_loop(0, 4, body, 0)

    def columns(h, s):
        row = ordv[h // 3, h % 3 : h % 3 + 1, :]
        oc[s] = jnp.broadcast_to(row, (128, 1024)).T

    def sort_mat(s, r):
        b = oc[s, rows_of(r, 128), :]
        return jnp.concatenate(
            [jnp.where(b == lane + 128 * k, 1.0, 0.0).astype(BF) for k in range(8)], axis=1
        )

    def unsort_mat(h, r):
        row = ordv[h // 3, h % 3 : h % 3 + 1, :]
        return jnp.where(sub + 128 * r == row, 1.0, 0.0).astype(BF)

    def attend(i):
        for s in range(2):
            h = 2 * i + s
            columns(h, s)

            def body(r, _, s=s, h=h):
                got = mm(sort_mat(s, r), qkv[i, :, 128 * s : 128 * s + 256])
                if s == 0:
                    kv = got[:, 0:128].astype(BF)
                    q = jnp.where(low, got[:, 128:256], 0.0).astype(BF)
                else:
                    q = jnp.where(low, 0.0, got[:, 0:128]).astype(BF)
                    kv = got[:, 128:256].astype(BF)
                rr = rows_of(r, 128)
                sq[h, rr, :] = q
                skv[h, rr, :] = kv
                sc = mm(q, kv, NT) * 0.125
                top = jnp.max(sc, axis=-1, keepdims=True)
                ex = jnp.exp(sc - top)
                prob = ex / jnp.sum(ex, axis=-1, keepdims=True)
                pr[h, rr, :] = prob
                mx = mm(prob.astype(BF), kv)
                ms[s, rr, 0:128] = (
                    jnp.where(low, 0.0, mx) if s == 0 else jnp.where(low, mx, 0.0)
                ).astype(BF)
                return 0

            lax.fori_loop(0, 8, body, 0)

        def back(r, _):
            both = mm(unsort_mat(2 * i, r), ms[0, :, 0:128]) + mm(
                unsort_mat(2 * i + 1, r), ms[1, :, 0:128]
            )
            mix[rows_of(r, 128), 128 * i : 128 * i + 128] = both.astype(BF)
            return 0

        lax.fori_loop(0, 8, back, 0)

    attend(0)
    w_fwd(1)
    w_fwd2(1)
    attend(1)
    w_fwd(2)
    w_fwd2(2)
    attend(2)

    mine = 512 * c
    other = 512 - mine

    def at(off, m, n):
        return pl.ds(pl.multiple_of(off + m * n, n), n)

    def partial(fn, k):
        if k >= 2:
            wait_send(snd.at[k % 2], pe_s.at[k - 2])
        for m in range(2):
            snd[k % 2, pl.ds(256 * m, 256), :] = fn(at(other, m, 256)).astype(BF)
        rc(snd.at[k % 2], rcv.at[k], pe_s.at[k], pe_r.at[k], (sib, z)).start()
        for m in range(2):
            op[pl.ds(256 * m, 256), :] = fn(at(mine, m, 256))
        wait_recv(rcv.at[k], pe_r.at[k])

    def share(ref, k):
        own = ref.at[pl.ds(pl.multiple_of(mine, 512), 512)]
        rc(own, own, pe_s.at[4 + k], pe_r.at[4 + k], (sib, z)).start()

    def shared(ref, k):
        wait_recv(ref.at[pl.ds(pl.multiple_of(other, 512), 512)], pe_r.at[4 + k])

    partial(lambda rows: mm(mix[rows, :], wo[...], NT), 0)

    def norm1(m, _):
        rr = rows_of(m, 128)
        v = (
            xall[2 * c + m // 2, pl.ds(pl.multiple_of(128 * lax.rem(m, 2), 128), 128), :].astype(F32)
            + op[rr, :]
            + rcv[0, rr, :].astype(F32)
            + par[0:1, :]
        )
        cen = v - jnp.mean(v, axis=-1, keepdims=True)
        rstd = lax.rsqrt(jnp.mean(cen * cen, axis=-1, keepdims=True) + NORM_EPS)
        nv = cen * rstd
        n1[rr, :] = nv
        rs1[rr, :] = rstd
        fv = nv * par[1:2, :] + par[2:3, :]
        fst[rr, :] = fv
        flow[at(mine, m, 128), :] = fv.astype(BF)
        return 0

    lax.fori_loop(0, 4, norm1, 0)
    share(flow, 0)
    w_done(1)
    w_done(2)

    def ffn_up(off):
        for u in range(2):

            def body(m, _, u=u):
                rr = at(off, m, 128)
                h = mm(flow[rr, :], wg[1, u]) + bias[u, 1:2, :]
                cdf = 0.5 + 0.5 * lax.erf(h * RSQRT2)
                act[rr, 768 * u : 768 * u + 768] = (h * cdf).astype(BF)
                dg[rr, 768 * u : 768 * u + 768] = (
                    cdf + h * (jnp.exp(-0.5 * h * h) * RSQRT2PI)
                ).astype(BF)
                return 0

            lax.fori_loop(0, 4, body, 0)

    ffn_up(mine)
    shared(flow, 0)
    ffn_up(other)
    partial(
        lambda rows: mm(act[rows, 0:768], wg[2, 0]) + mm(act[rows, 768:1536], wg[2, 1]), 1
    )

    vb[0] = jnp.zeros((16, 768), F32)
    ones8 = jnp.zeros((1, 768), F32)

    def norm2(m, carry):
        sgain, sshift, dbias = carry
        rr = rows_of(m, 128)
        v = fst[rr, :] + op[rr, :] + rcv[1, rr, :].astype(F32) + par[3:4, :]
        cen = v - jnp.mean(v, axis=-1, keepdims=True)
        rstd = lax.rsqrt(jnp.mean(cen * cen, axis=-1, keepdims=True) + NORM_EPS)
        nv = cen * rstd
        tok[rr, :] = (nv * par[4:5, :] + par[5:6, :]).astype(BF)
        pos = lax.broadcasted_iota(jnp.int32, (128, 256), 0) + (mine + 128 * m)
        hits = jnp.where(pos == mr[0:1, :], 1.0, 0.0).astype(BF)
        dout = mm(hits, mg[...])
        gg = dout * par[4:5, :]
        d2 = (
            gg
            - jnp.mean(gg, axis=-1, keepdims=True)
            - nv * jnp.mean(gg * nv, axis=-1, keepdims=True)
        ) * rstd
        fst[rr, :] = d2
        dlo = d2.astype(BF)
        dl[at(mine, m, 128), :] = dlo
        return (
            sgain + jnp.sum(dout * nv, axis=0, keepdims=True),
            sshift + jnp.sum(dout, axis=0, keepdims=True),
            dbias + jnp.sum(dlo.astype(F32), axis=0, keepdims=True),
        )

    sg, ss, db = lax.fori_loop(0, 4, norm2, (ones8, ones8, ones8))
    share(dl, 1)
    vb[0, 0:1, :] = sg
    vb[0, 1:2, :] = ss
    vb[0, 2:3, :] = db

    def tok_send(src, dst, k):
        for u in range(2):
            self_ = prim & (z == 2 * c + u)
            s_ = src.at[pl.ds(256 * u, 256)]
            d_ = dst.at[zj]

            @pl.when(self_)
            def _(s_=s_, d_=d_):
                lc(s_, d_, t_l.at[k]).start()

            @pl.when(jnp.logical_not(self_))
            def _(s_=s_, d_=d_, u=u):
                rc(s_, d_, t_s.at[k, u], t_r.at[k, zj], (base + zc, 2 * c + u)).start()

    def tok_wait(src, dst, k):
        for j in range(2):
            loc = prim & (z == 2 * c + j)

            @pl.when(loc)
            def _(j=j):
                lc(src.at[pl.ds(0, 256)], dst.at[j], t_l.at[k]).wait()

            @pl.when(jnp.logical_not(loc))
            def _(j=j):
                wait_recv(dst.at[j], t_r.at[k, j])
                wait_send(src.at[pl.ds(0, 256)], t_s.at[k, j])

    tok_send(tok, o1, 0)

    def g_start(a, u):
        for r in range(2):
            p1, p2 = pp(r)
            src = g.at[a, u, pl.ds(pl.multiple_of(384 * r + 192 * (1 - p1), 64), 192)]
            rc(src, st1.at[a, u, r], g1_s.at[a, u, r], g1_r.at[a, u, r], nbs(r)[0]).start()

    def quarter(ref, r, q):
        return ref.at[pl.ds(pl.multiple_of(96 * q, 32), 96)]

    def g_step2(a, u):
        for r in range(2):
            p1, p2 = pp(r)
            wait_recv(st1.at[a, u, r], g1_r.at[a, u, r])
            rows = blk(r, p1, 1 - p2)
            part = st1[a, u, r, pl.ds(pl.multiple_of(96 * (1 - p2), 32), 96), :]
            g[a, u, rows, :] = (g[a, u, rows, :].astype(F32) + part.astype(F32)).astype(BF)
            rc(
                g.at[a, u, rows], st2.at[a, u, r], g2_s.at[a, u, r], g2_r.at[a, u, r], nbs(r)[1]
            ).start()

    def g_step3(a, u):
        for r in range(2):
            p1, p2 = pp(r)
            wait_recv(st2.at[a, u, r], g2_r.at[a, u, r])
            rows = blk(r, p1, p2)
            part = st1[a, u, r, pl.ds(pl.multiple_of(96 * p2, 32), 96), :]
            tot = (
                g[a, u, rows, :].astype(F32) + part.astype(F32) + st2[a, u, r].astype(F32)
            ).astype(BF)
            self_ = (c == r) & (z == 2 * c + u)

            @pl.when(self_)
            def _(tot=tot):
                st3[a, z] = tot

            @pl.when(jnp.logical_not(self_))
            def _(tot=tot, rows=rows, r=r):
                g[a, u, rows, :] = tot
                rc(
                    g.at[a, u, rows], st3.at[a, z], g3_s.at[a, u, r], g3_r.at[a, z],
                    (base + r, 2 * c + u),
                ).start()

    q1 = px + c * (py - px)
    q2 = py + c * (px - py)
    e1 = (xn + c * (yn - xn), z)
    e2 = (yn + c * (xn - yn), z)

    def own(r, p1, p2):
        return pl.ds(pl.multiple_of(384 * r + 96 * (2 * p1 + p2), 32), 96)

    def g_step4(a):
        for k in range(4):
            loc = prim & (z == k)

            @pl.when(jnp.logical_not(loc))
            def _(k=k):
                wait_recv(st3.at[a, k], g3_r.at[a, k])

        rb[a] = (
            st3[a, 0].astype(F32)
            + st3[a, 1].astype(F32)
            + st3[a, 2].astype(F32)
            + st3[a, 3].astype(F32)
        ).astype(BF)
        dst = res.at[a, own(c, q1, q2)]
        rc(rb.at[a], dst, ag_s.at[a, 0], ag_r.at[a, 0], e1).start()
        rc(rb.at[a], dst, ag_s.at[a, 1], ag_r.at[a, 1], e2).start()
        rc(rb.at[a], dst, ce_s.at[a, 0], ce_r.at[a, 0], (sib, z)).start()
        lc(rb.at[a], dst, ag_l.at[a]).start()

    def g_step5(a):
        ref = res.at[a, own(c, 1 - q1, q2)]
        wait_recv(ref, ag_r.at[a, 0])
        rc(ref, ref, ag_s.at[a, 2], ag_r.at[a, 2], e2).start()
        rc(ref, ref, ce_s.at[a, 1], ce_r.at[a, 1], (sib, z)).start()

    def g_step6(a):
        ref = res.at[a, own(c, q1, 1 - q2)]
        wait_recv(ref, ag_r.at[a, 1])
        rc(ref, ref, ce_s.at[a, 2], ce_r.at[a, 2], (sib, z)).start()
        ref = res.at[a, own(c, 1 - q1, 1 - q2)]
        wait_recv(ref, ag_r.at[a, 2])
        rc(ref, ref, ce_s.at[a, 3], ce_r.at[a, 3], (sib, z)).start()

    def g_end(a):
        lc(rb.at[a], res.at[a, own(c, q1, q2)], ag_l.at[a]).wait()
        o_ = 1 - c
        for k, rows in enumerate(
            (own(o_, q2, q1), own(o_, 1 - q2, q1), own(o_, q2, 1 - q1), own(o_, 1 - q2, 1 - q1))
        ):
            wait_recv(res.at[a, rows], ce_r.at[a, k])
            wait_send(rb.at[a], ce_s.at[a, k])
        for k in range(3):
            wait_send(rb.at[a], ag_s.at[a, k])
        for u in range(2):
            for r in range(2):
                wait_send(st1.at[a, u, r], g1_s.at[a, u, r])
                wait_send(st2.at[a, u, r], g2_s.at[a, u, r])

                @pl.when(jnp.logical_not((c == r) & (z == 2 * c + u)))
                def _(u=u, r=r):
                    wait_send(st2.at[a, u, r], g3_s.at[a, u, r])

    shared(dl, 1)

    def tmm(dst_fn, lhs_fn, rhs_fn, n):
        def body(m, _):
            dst_fn(m, mm(lhs_fn(m), rhs_fn(), TN))
            return 0

        lax.fori_loop(0, n, body, 0)

    for u in range(2):
        for n in range(3):
            cols = slice(768 * u + 256 * n, 768 * u + 256 * n + 256)
            g[2, u, 256 * n : 256 * n + 256, :] = mm(act[:, cols], dl[...], TN).astype(BF)
        g_start(2, u)

    for u in range(2):

        def dup(m, carry, u=u):
            rr = rows_of(m, 128)
            cols = slice(768 * u, 768 * u + 768)
            dv = (mm(dl[rr, :], wg[2, u], NT) * dg[rr, cols].astype(F32)).astype(BF)
            dg[rr, cols] = dv
            return carry + jnp.sum(dv.astype(F32), axis=0, keepdims=True)

        ub = lax.fori_loop(0, 8, dup, jnp.zeros((1, 768), F32))
        vb[0, pl.ds(6 + 2 * c + u, 1), :] = ub
    for u in range(2):
        g_step2(2, u)
    partial(
        lambda rows: mm(dg[rows, 0:768], wg[1, 0], NT) + mm(dg[rows, 768:1536], wg[1, 1], NT), 2
    )
    for u in range(2):
        for n in range(3):
            g[1, u, 256 * n : 256 * n + 256, :] = mm(
                flow[:, 256 * n : 256 * n + 256], dg[:, 768 * u : 768 * u + 768], TN
            ).astype(BF)
        g_start(1, u)
    for u in range(2):
        g_step3(2, u)

    def norm1b(m, carry):
        fg, fs, ob = carry
        rr = rows_of(m, 128)
        df = fst[rr, :] + op[rr, :] + rcv[2, rr, :].astype(F32)
        nv = n1[rr, :]
        gg = df * par[1:2, :]
        dr = (
            gg
            - jnp.mean(gg, axis=-1, keepdims=True)
            - nv * jnp.mean(gg * nv, axis=-1, keepdims=True)
        ) * rs1[rr, :]
        fst[rr, :] = dr
        dlo = dr.astype(BF)
        da[at(mine, m, 128), :] = dlo
        return (
            fg + jnp.sum(df * nv, axis=0, keepdims=True),
            fs + jnp.sum(df, axis=0, keepdims=True),
            ob + jnp.sum(dlo.astype(F32), axis=0, keepdims=True),
        )

    fg, fs, ob = lax.fori_loop(0, 4, norm1b, (ones8, ones8, ones8))
    share(da, 2)
    vb[0, 3:4, :] = fg
    vb[0, 4:5, :] = fs
    vb[0, 5:6, :] = ob
    for u in range(2):
        g_step2(1, u)
    shared(da, 2)

    def dmix(m, _):
        rr = rows_of(m, 256)
        dm[rr, :] = mm(da[rr, :], wo[...]).astype(BF)
        return 0

    lax.fori_loop(0, 4, dmix, 0)
    for n in range(3):
        gw = mm(da[:, 256 * n : 256 * n + 256], mix[...], TN)
        rows = slice(256 * n, 256 * n + 256)
        g[0, 0, rows, 512:640] = gw[:, 0:128].astype(BF)
        g[0, 1, rows, 512:640] = gw[:, 256:384].astype(BF)
        wm_ = gw[:, 128:256].astype(BF)
        g[0, 0, rows, 640:768] = wm_
        g[0, 1, rows, 640:768] = wm_

    def attend_back(i):
        for s in range(2):
            h = 2 * i + s
            columns(h, s)

            def body(r, _, s=s, h=h):
                rr = rows_of(r, 128)
                uu = mm(sort_mat(s, r), dm[:, 128 * i : 128 * i + 128])
                uu = (jnp.where(low, 0.0, uu) if s == 0 else jnp.where(low, uu, 0.0)).astype(BF)
                kv = skv[h, rr, :]
                q = sq[h, rr, :]
                prob = pr[h, rr, :]
                dp = mm(uu, kv, NT)
                cen = jnp.sum(prob * dp, axis=-1, keepdims=True)
                ds = (prob * (dp - cen)).astype(BF)
                dq = mm(ds, kv) * 0.125
                dkv = mm(prob.astype(BF), uu, TN) + mm(ds, q, TN) * 0.125
                if s == 0:
                    ms[s, rr, 0:128] = dkv.astype(BF)
                    ms[s, rr, 128:256] = jnp.where(low, dq, 0.0).astype(BF)
                else:
                    ms[s, rr, 0:128] = jnp.where(low, 0.0, dq).astype(BF)
                    ms[s, rr, 128:256] = dkv.astype(BF)
                return 0

            lax.fori_loop(0, 8, body, 0)

        def back(r, carry):
            ga = mm(unsort_mat(2 * i, r), ms[0])
            gb = mm(unsort_mat(2 * i + 1, r), ms[1])
            out = jnp.concatenate(
                [ga[:, 0:128], ga[:, 128:256] + gb[:, 0:128], gb[:, 128:256]], axis=1
            )
            qkv[i, rows_of(r, 128), :] = out.astype(BF)
            return carry + jnp.sum(out, axis=0, keepdims=True)

        return lax.fori_loop(0, 8, back, jnp.zeros((1, 384), F32))

    def gqkv(i):
        for n in range(3):
            rows = slice(256 * n, 256 * n + 256)
            gw = mm(
                jnp.concatenate([xall[k, :, rows] for k in range(4)], axis=0), qkv[i], TN
            )
            if i != 1:
                g[0, i // 2, rows, 0:384] = gw.astype(BF)
            else:
                g[0, 0, rows, 384:512] = gw[:, 0:128].astype(BF)
                g[0, 1, rows, 384:512] = gw[:, 256:384].astype(BF)
                lo = low1
                t0 = g[0, 0, rows, 640:768].astype(F32)
                g[0, 0, rows, 640:768] = jnp.where(lo, gw[:, 128:256], t0).astype(BF)
                g[0, 1, rows, 640:768] = jnp.where(lo, t0, gw[:, 128:256]).astype(BF)

    b0 = attend_back(0)
    gqkv(0)
    for u in range(2):
        g_step3(1, u)
    b1 = attend_back(1)
    gqkv(1)
    g_step4(2)
    g_start(0, 0)
    b2 = attend_back(2)
    gqkv(2)
    g_start(0, 1)
    zero = jnp.zeros((1, 128), F32)
    vb[0, pl.ds(10 + 2 * c, 1), :] = jnp.concatenate([b0, b1[:, 0:128], zero, b1[:, 128:256]], axis=1)
    vb[0, pl.ds(11 + 2 * c, 1), :] = jnp.concatenate(
        [b2, b1[:, 256:384], zero, b1[:, 128:256]], axis=1
    )

    vdev = (
        (sib, z), (xn, z), (yn, z), (d, z + 1 - 2 * zj), (d, z + 2 - 4 * zc),
    )

    def v_send(k):
        rc(vb.at[k], vr.at[k], v_s.at[k], v_r.at[k], vdev[k]).start()

    def v_add(k):
        wait_recv(vr.at[k], v_r.at[k])
        vb[k + 1] = vb[k] + vr[k]

    v_send(0)
    partial(
        lambda rows: mm(qkv[0, rows, :], wq(0), NT)
        + mm(qkv[1, rows, :], wq(1), NT)
        + mm(qkv[2, rows, :], wq(2), NT),
        3,
    )

    def gin(m, _):
        rr = rows_of(m, 128)
        gtok[rr, :] = (fst[rr, :] + op[rr, :] + rcv[3, rr, :].astype(F32)).astype(BF)
        return 0

    lax.fori_loop(0, 4, gin, 0)
    tok_send(gtok, o2, 1)
    g_step5(2)
    g_step4(1)
    v_add(0)
    v_send(1)
    g_step2(0, 0)
    g_step2(0, 1)
    g_step6(2)
    g_step5(1)
    v_add(1)
    v_send(2)
    g_step6(1)
    g_step3(0, 0)
    g_step3(0, 1)
    v_add(2)
    v_send(3)
    g_step4(0)
    v_add(3)
    v_send(4)
    g_step5(0)
    v_add(4)
    vout[...] = vb[5]
    g_step6(0)
    for a in range(3):
        g_end(a)
    tok_wait(tok, o1, 0)
    tok_wait(gtok, o2, 1)

    for a in range(3):
        w_end(a)
    for k in range(4):
        wait_send(xall.at[k, crows], cx_s.at[k])
        if k >= 2:
            wait_send(rcv.at[k], pe_s.at[k])
    for k in range(3):
        wait_send(flow.at[pl.ds(0, 512)], pe_s.at[4 + k])
    for k in range(5):
        wait_send(vb.at[k], v_s.at[k])
    for j in range(2):

        @pl.when(jnp.logical_not(prim & (z == 2 * c + j)))
        def _(j=j):
            wait_send(ord_in.at[j], o_s.at[j])

        for h in range(2):

            @pl.when(jnp.logical_not((c == h) & (z == 2 * c + j)))
            def _(j=j, h=h):
                wait_send(x_in.at[j, pl.ds(0, 128)], x_s.at[j, h])

    @pl.when(prim)
    def _():
        for k in range(3):
            wait_send(bias_in, b_s.at[k])
        wait_send(mr_in.at[0], m_s.at[0])
        wait_send(mg_in.at[0], m_s.at[1])


def layer(x, order, wa, wb, wc, bias, par, mr, mg):
    dma = pltpu.SemaphoreType.DMA
    hbm = pl.BlockSpec(memory_space=pl.ANY)
    vmem = pl.BlockSpec(memory_space=pltpu.VMEM)
    V = pltpu.VMEM
    return pl.pallas_call(
        kernel,
        out_shape=(
            jax.ShapeDtypeStruct((2, 256, 768), BF),
            jax.ShapeDtypeStruct((2, 256, 768), BF),
            jax.ShapeDtypeStruct((3, 768, 768), BF),
            jax.ShapeDtypeStruct((16, 768), F32),
        ),
        in_specs=[hbm, hbm, hbm, hbm, hbm, hbm, vmem, hbm, hbm],
        out_specs=(hbm, hbm, hbm, vmem),
        scratch_shapes=[
            V((4, 256, 768), BF),
            V((2, 8, 1024), jnp.int32),
            V((3, 2, 768, 768), BF),
            V((2, 8, 768), F32),
            V((8, 256), jnp.int32),
            V((256, 768), BF),
            V((768, 384), BF),
            V((768, 384), BF),
            V((3, 1024, 384), BF),
            V((2, 1024, 128), jnp.int32),
            V((6, 1024, 128), BF),
            V((6, 1024, 128), BF),
            V((6, 1024, 128), F32),
            V((2, 1024, 256), BF),
            V((1024, 384), BF),
            V((2, 512, 768), BF),
            V((4, 512, 768), BF),
            V((512, 768), F32),
            V((512, 768), F32),
            V((512, 768), F32),
            V((512, 1), F32),
            V((1024, 768), BF),
            V((1024, 1536), BF),
            V((1024, 1536), BF),
            V((1024, 768), BF),
            V((1024, 768), BF),
            V((1024, 384), BF),
            V((3, 2, 768, 768), BF),
            V((3, 2, 2, 192, 768), BF),
            V((3, 2, 2, 96, 768), BF),
            V((3, 4, 96, 768), BF),
            V((3, 96, 768), BF),
            V((512, 768), BF),
            V((512, 768), BF),
            V((6, 16, 768), F32),
            V((5, 16, 768), F32),
            dma((2, 2)), dma((4,)), dma, dma((4,)), dma((4,)),
            dma((2,)), dma((2,)), dma,
            dma((3,)), dma((2,)), dma,
            dma((2,)), dma((2,)), dma((2,)),
            dma((3, 2, 2)), dma((3, 2)), dma((3, 2, 2)),
            dma((3, 2, 2, 3)), dma((3, 2, 2, 3)), dma((3,)),
            dma((7,)), dma((7,)),
            dma((2, 2)), dma((2, 2)), dma((2,)),
            dma((5,)), dma((5,)),
            dma((3, 2, 2)), dma((3, 2, 2)), dma((3, 2, 2)), dma((3, 2, 2)),
            dma((3, 2, 2)), dma((3, 4)), dma((3, 3)), dma((3, 3)), dma((3,)),
            dma((3, 4)), dma((3, 4)),
        ],
        compiler_params=pltpu.CompilerParams(
            collective_id=0, has_side_effects=True, vmem_limit_bytes=60 * 2**20
        ),
    )(x, order, wa, wb, wc, bias, par, mr, mg)


def split64(a, n):
    return [a[..., 64 * k : 64 * k + 64] for k in range(n)]


def shards(
    inputs, qkv_weight, qv_bias, out_weight, out_bias, first_gain, first_shift,
    first_layer_weight, first_layer_bias, second_layer_weight, second_layer_bias,
    second_gain, second_shift, cluster_order, masked_rows, masked_grad,
):
    t = lax.axis_index("tensor")
    even = lax.rem(t, 2) == 0

    q = split64(qkv_weight[:, 0], 3)
    k = split64(qkv_weight[:, 1], 3)
    v = split64(qkv_weight[:, 2], 3)
    o = split64(out_weight.T, 3)

    def arrange(q, k, v, o):
        ev = [k[0], v[0], q[0], q[1], v[1], k[1], k[2], v[2], o[1], o[0], q[2], o[2]]
        od = [k[1], v[1], q[1], q[2], v[2], k[2], v[0], k[0], o[2], o[1], o[0], q[0]]
        return jnp.where(even, jnp.concatenate(ev, axis=-1), jnp.concatenate(od, axis=-1))

    wa = arrange(q, k, v, o)
    zs = [jnp.zeros((64,), BF)] * 3
    bias_a = arrange(split64(qv_bias[0], 3), zs, split64(qv_bias[1], 3), zs)
    bias = jnp.zeros((8, 768), F32).at[0].set(bias_a.astype(F32)).at[1].set(
        first_layer_bias.astype(F32)
    )
    nil = jnp.zeros((768,), BF)
    par = jnp.stack(
        [out_bias, first_gain, first_shift, second_layer_bias, second_gain, second_shift, nil, nil]
    ).astype(F32)
    order = jnp.pad(cluster_order, ((0, 0), (0, 5), (0, 0)))
    masked = masked_rows.shape[1]
    mr = jnp.pad(masked_rows, ((0, 0), (0, 256 - masked)), constant_values=-1)
    mr = jnp.broadcast_to(mr[:, None, :], (2, 8, 256))
    mg = jnp.pad(masked_grad, ((0, 0), (0, 256 - masked), (0, 0)))
    x = inputs.transpose(1, 0, 2)

    o1, o2, res, vec = layer(
        x, order, wa, first_layer_weight, second_layer_weight, bias, par, mr, mg
    )

    many = lax.axis_size("dp") // 8
    if many > 1:
        groups = [[8 * i + j for i in range(many)] for j in range(8)]
        res = lax.psum(res.astype(F32), "dp", axis_index_groups=groups)
        vec = lax.psum(vec, "dp", axis_index_groups=groups)
    res = res.astype(F32)
    outputs = o1.transpose(1, 0, 2)
    grad_inputs = o2.transpose(1, 0, 2).astype(F32)

    def restore(a):
        b = split64(a, 12)
        ev = [b[2], b[3], b[10], b[0], b[5], b[6], b[1], b[4], b[7], b[9], b[8], b[11]]
        od = [b[11], b[2], b[3], b[7], b[0], b[5], b[6], b[1], b[4], b[10], b[9], b[8]]
        both = jnp.where(even, jnp.concatenate(ev, axis=-1), jnp.concatenate(od, axis=-1))
        return both[..., 0:576], both[..., 576:768]

    gq, go = restore(res[0])
    row = lax.dynamic_slice_in_dim(vec, 10 + t, 1, 0)
    gb = restore(row)[0].reshape(3, 192)
    return (
        outputs,
        grad_inputs,
        gq.reshape(768, 3, 192),
        jnp.stack([gb[0], gb[2]]),
        go.T,
        vec[5],
        vec[3],
        vec[4],
        res[1],
        lax.dynamic_slice_in_dim(vec, 6 + t, 1, 0)[0],
        res[2],
        vec[2],
        vec[0],
        vec[1],
    )


def solution(mesh):
    placed = (
        P("tensor", "dp", None), P(None, None, "tensor"), P(None, "tensor"), P("tensor", None),
        P(), P(), P(), P(None, "tensor"), P("tensor"), P("tensor", None), P(), P(), P(),
        P("dp", "tensor", None), P("dp", None), P("dp", None, None),
    )
    return jax.shard_map(
        shards,
        mesh=mesh,
        in_specs=placed,
        out_specs=(
            P("tensor", "dp", None), P("tensor", "dp", None), P(None, None, "tensor"),
            P(None, "tensor"), P("tensor", None), P(), P(), P(), P(None, "tensor"), P("tensor"),
            P("tensor", None), P(), P(), P(),
        ),
        check_vma=False,
    )
```

time: 1280 us -> 309 us (0.24)
  waiting for transfers between devices: 677 us -> 0 us
  local copies, waits for them, and re-layouts: 379 us -> 38 us
  Pallas kernels: 0 us -> 258 us
  matrix products: 77 us -> 0 us
  blocking collectives: 59.3 us -> 0 us
  other arithmetic: 56.9 us -> 8.24 us
  between operations: 14.7 us -> 1.24 us
    reduce_scatter x4 -> x0, waiting for transfers between devices: 335 us -> none  [the longest x1 112 us: shards(): lax.psum_scatter(jnp.einsum('qrh,ah->qra', picked_tokens, first_layer_wei...]
    pallas_call x0 -> x1, Pallas kernels: none -> 258 us  [layer(): pl.pallas_call(kernel, out_shape=(jax.ShapeDtypeStruct((2, 256, 768), BF)...]
    all_gather x4 -> x0, waiting for transfers between devices: 246 us -> none  [the longest x1 62.2 us: shards(): inputs_all = lax.all_gather(inputs, 'tensor', axis=0, tiled=True)]
    gather x32 -> x0, local copies, waits for them, and re-layouts: 238 us -> none  [sort_heads(): jnp.take(block, picks, axis=0)]
    psum x1 -> x0, waiting for transfers between devices: 95.3 us -> none  [shards(): lax.psum((grad_qkvweight, grad_qvbias, grad_outweight, grad_upweight, gra...]
    while x69 -> x0, local copies, waits for them, and re-layouts: 79.3 us -> none
    dot_general x23 -> x0, matrix products: 70.7 us -> none  [the longest x1 11.1 us: shards(): jnp.einsum('eah,jh->eaj', lowered_gradient_full, second_layer_weight, pre...]
    psum x2 -> x0, blocking collectives: 59.3 us -> none  [the longest x1 45.8 us: shards(): lax.psum((grad_outbias, grad_firstgain, grad_firstshift, grad_downbias, g...]
  transfers between devices with their start and end apart: 9 -> 0, of which waited for: 8 -> 0; matrix products, arithmetic and copies ran while one was open for 2% -> 0% of each run, Pallas kernels for 0% -> 0%
where the time goes in v1:
time: 309 us; the launch traced here: 306 us
  Pallas kernels  258 us (83%)
  local copies, waits for them, and re-layouts  38 us (12%)
  other arithmetic  8.24 us (3%)
    pallas_call x1, Pallas kernels, layer(): pl.pallas_call(kernel, out_shape=(jax.ShapeDtypeStruct((2, 256, 768), BF)...  258 us
    unnamed x40, local copies, waits for them, and re-layouts  7.93 us

profile of v1, /device:TPU:9, one launch (start us, length us, event | category | flops | bytes accessed | tf_op | source)
XLA Modules:
  0.0 305.6 jit_solution(3727745565481364084)
XLA Ops:
  0.6 1.2 fusion.2
  2.2 0.9 fusion.3
  3.8 0.8 fusion.5
  4.5 2.2 concatenate.68
  6.7 0.8 slice.294
  7.5 2.3 concatenate.67
  9.9 1.1 broadcast_select_fusion.1.wa_in
  11.6 1.1 copy.47
  12.7 0.9 pad.20.mg_in
  13.6 1.0 copy.56
  14.6 0.6 pad.18.ord_in
  15.4 0.6 convert_element_type.21.par
  16.0 0.6 broadcast_in_dim.5.mr_in
  16.6 258.1 %shard_map.263 = (bf16[2,256,768]{2,1,0:T(8,128)(2,1)}, bf16[2,256,768]{2,1,0:T(8,128)(2,1)}, bf16[3,768,768]{2,1,0:T(8,128)(2,1)}, f32[16,768]{1,0:T(8,128)}) custom-call(bf16[2,256,768]{2,1,0:T(8,128)(2,1)} %bitcast.23, s32[2,8,1024]{2,1,0:T(8,128)} %pad.18.ord_in, bf16[768,768]{1,0:T(8,128)(2,1)} %broadcast_select_fusion.1.wa_in, bf16[768,768]{1,0:T(8,128)(2,1)} %wb_in.1, ...), custom_call_target="tpu_custom_call" | custom-call | tf_op jit(solution)/shard_map/pallas_call | solution.py:857
  274.7 0.9 fusion.8
  275.6 0.8 fusion.9
  276.6 0.6 pad_maximum_fusion
  277.2 2.6 convert_element_type.24
  279.8 2.6 slice_bitcast_fusion
  282.4 0.5 fusion
  282.9 0.9 fusion.1
  283.8 3.7 %concatenate.74 = f32[768,768]{1,0:T(8,128)} concatenate(f32[768,64]{1,0:T(8,128)S(1)} %get-tuple-element.84, f32[768,128]{1,0:T(8,128)} %get-tuple-element.93, f32[768,64]{1,0:T(8,128)S(1)} %get-tuple-element.87, f32[768,64]{1,0:T(8,128)S(1)} %get-tuple-element.90, f32[768,128]{1,0:T(8,128)S(1)} %get-tuple-element.92, f32[768,64]{1,0:T(8,128)S(1)} %get-tuple-element.89, ...), dimensions={1} | concatenate | bytes 4718592 | tf_op jit(solution)/shard_map/concatenate | solution.py:979
  287.4 3.2 %concatenate.73 = f32[768,768]{1,0:T(8,128)} concatenate(f32[768,128]{1,0:T(8,128)} %get-tuple-element.93, f32[768,64]{1,0:T(8,128)S(1)} %get-tuple-element.91, f32[768,64]{1,0:T(8,128)S(1)} %get-tuple-element.90, f32[768,128]{1,0:T(8,128)S(1)} %get-tuple-element.92, f32[768,64]{1,0:T(8,128)S(1)} %get-tuple-element.89, f32[768,64]{1,0:T(8,128)S(1)} %get-tuple-element.88, ...), dimensions={1} | concatenate | bytes 4718592 | tf_op jit(solution)/shard_map/concatenate | solution.py:979
  290.7 2.0 broadcast_select_fusion
  292.6 1.4 slice.315
  294.1 2.8 copy.48
  296.8 0.3 slice_bitcast_fusion.3
  297.1 1.1 copy.51
  298.2 1.3 convert_bitcast_fusion
  299.5 2.4 copy.50
  301.9 1.7 copy.49
  303.5 1.8 slice_reduce_fusion
  (60 shorter events, 1.8 us)
Async XLA Ops:
  1.8 1.5 copy-start.3
  3.1 3.6 %copy-start = (bf16[768,64]{1,0:T(8,128)(2,1)}, bf16[768,64]{1,0:T(8,128)(2,1)S(1)}, u32[]{:S(2)}) copy-start(bf16[768,64]{1,0:T(8,128)(2,1)S(1)} %get-tuple-element.129) | copy-start | bytes 294916
  9.8 1.2 copy-start.6
  9.8 1.6 copy-start.7
  9.8 3.8 %copy-start.1 = (bf16[256,2,768]{2,1,0:T(2,128)(2,1)S(1)}, bf16[256,2,768]{2,1,0:T(2,128)(2,1)}, u32[]{:S(2)}) copy-start(bf16[256,2,768]{2,1,0:T(2,128)(2,1)} %param.20) | copy-start | bytes 2359300
  11.0 3.6 %copy-start.5 = (s32[2,3,1024]{2,0,1:T(2,128)S(1)}, s32[2,3,1024]{2,0,1:T(2,128)}, u32[]{:S(2)}) copy-start(s32[2,3,1024]{2,0,1:T(2,128)} %param.33) | copy-start | bytes 73732
  11.0 4.2 %copy-start.8 = (bf16[768]{0:T(1024)(128)(2,1)S(1)}, bf16[768]{0:T(1024)(128)(2,1)}, u32[]{:S(2)}) copy-start(bf16[768]{0:T(1024)(128)(2,1)} %param.24) | copy-start | bytes 4612
  11.0 4.2 %copy-start.9 = (bf16[768]{0:T(1024)(128)(2,1)S(1)}, bf16[768]{0:T(1024)(128)(2,1)}, u32[]{:S(2)}) copy-start(bf16[768]{0:T(1024)(128)(2,1)} %param.25) | copy-start | bytes 4612
  11.0 4.2 %copy-start.10 = (bf16[768]{0:T(1024)(128)(2,1)S(1)}, bf16[768]{0:T(1024)(128)(2,1)}, u32[]{:S(2)}) copy-start(bf16[768]{0:T(1024)(128)(2,1)} %param.26) | copy-start | bytes 4612
  11.0 4.3 %copy-start.11 = (bf16[768]{0:T(1024)(128)(2,1)S(1)}, bf16[768]{0:T(1024)(128)(2,1)}, u32[]{:S(2)}) copy-start(bf16[768]{0:T(1024)(128)(2,1)} %param.30) | copy-start | bytes 4612
  11.0 4.3 %copy-start.12 = (bf16[768]{0:T(1024)(128)(2,1)S(1)}, bf16[768]{0:T(1024)(128)(2,1)}, u32[]{:S(2)}) copy-start(bf16[768]{0:T(1024)(128)(2,1)} %param.31) | copy-start | bytes 4612
  11.0 4.3 %copy-start.13 = (bf16[768]{0:T(1024)(128)(2,1)S(1)}, bf16[768]{0:T(1024)(128)(2,1)}, u32[]{:S(2)}) copy-start(bf16[768]{0:T(1024)(128)(2,1)} %param.32) | copy-start | bytes 4612
  11.1 5.0 %copy-start.14 = (s32[2,154]{1,0:T(2,128)S(1)}, s32[2,154]{1,0:T(2,128)}, u32[]{:S(2)}) copy-start(s32[2,154]{1,0:T(2,128)} %param.34) | copy-start | bytes 3700
  11.6 5.1 %copy-start.4 = (f32[8,768]{1,0:T(8,128)}, f32[8,768]{1,0:T(8,128)S(1)}, u32[]{:S(2)}) copy-start(f32[8,768]{1,0:T(8,128)S(1)} %scatter.14.bias_in) | copy-start | bytes 73732
  298.2 3.7 %copy-start.2 = (bf16[2,256,768]{2,1,0:T(8,128)(2,1)S(1)}, bf16[2,256,768]{2,1,0:T(8,128)(2,1)}, u32[]{:S(2)}) copy-start(bf16[2,256,768]{2,1,0:T(8,128)(2,1)} %get-tuple-element.42) | copy-start | bytes 2359300

commit v2 on v1

v2 whole, which is shorter than its diff:
```python
import math

import jax
import jax.numpy as jnp
from jax import lax
from jax.experimental import pallas as pl
from jax.experimental.pallas import tpu as pltpu
from jax.sharding import PartitionSpec as P

HD = 64
C = 128
NORM_EPS = 1e-05
BF = jnp.bfloat16
F32 = jnp.float32
MESH = pl.DeviceIdType.MESH
RSQRT2 = 1.0 / math.sqrt(2.0)
RSQRT2PI = 1.0 / math.sqrt(2.0 * math.pi)

NN = (((1,), (0,)), ((), ()))
NT = (((1,), (1,)), ((), ()))
TN = (((0,), (0,)), ((), ()))


def mm(a, b, dims=NN):
    return lax.dot_general(a, b, dims, preferred_element_type=F32)


def kernel(
    x_in, ord_in, wq_in, wo_in, wb_in, wc_in, mr_in, mg_in, qb_in,
    p0, p1_, p2_, p3_, p4_, p5_, p6_,
    o1, o2, ra, rbb, rcc, vout,
    xall, x3, ordv, wg, bias, bias_in, par, mr, mg3, mg, wq, wo, qkv, oc, sq, skv, pr, mix,
    snd, rcv, op, fst, n1, rs1, flow, act, dg, dl, g, st1, st2, st3,
    rb, vb, vr,
    x_s, x_r, x_l, cx_s, cx_r, o_s, o_r, o_l, b_s, b_r, b_l, m_s, m_r, m_l,
    wz_s, wz_s2, wz_r, wx_s, wx_r, w_l, pe_s, pe_r, t_s, t_r, t_l, v_s, v_r,
    g1_s, g1_r, g2_s, g2_r, g3_s, g3_r, ag_s, ag_r, ag_l, ce_s, ce_r,
):
    w_in = (None, wb_in, wc_in)
    res = (ra, rbb, rcc)
    dm = act.at[:, 0:384]
    ms = (act.at[:, 512:768], act.at[:, 768:1024])
    tok = wg.at[0, 0, pl.ds(0, 512)]
    gtok = wg.at[0, 1, pl.ds(0, 512)]
    d = lax.axis_index("dp")
    z = lax.axis_index("tensor")
    c = lax.rem(d, 2)
    base = d - c
    sib = base + 1 - c
    px = lax.rem(lax.div(d, 2), 2)
    py = lax.rem(lax.div(d, 4), 2)
    xn = d + 2 - 4 * px
    yn = d + 4 - 8 * py
    zc = lax.div(z, 2)
    zj = lax.rem(z, 2)
    up = 1 - 2 * c
    zz = 3 * c + z * up
    prim = zc == c

    def rc(src, dst, ss, rs, dev):
        return pltpu.make_async_remote_copy(
            src_ref=src, dst_ref=dst, send_sem=ss, recv_sem=rs,
            device_id=dev, device_id_type=MESH,
        )

    def wait_send(src, ss):
        rc(src, src, ss, ss, (sib, z)).wait_send()

    def wait_recv(dst, rs):
        rc(dst, dst, rs, rs, (sib, z)).wait_recv()

    def lc(src, dst, sem):
        return pltpu.make_async_copy(src, dst, sem)

    bar = pltpu.get_barrier_semaphore()
    for k in range(1, 8):
        oc_, oz = k % 2, k // 2
        dev = (base + lax.rem(c + oc_, 2), lax.rem(z + oz, 4))
        pl.semaphore_signal(bar, inc=1, device_id=dev, device_id_type=MESH)
    for dev in ((xn, z), (yn, z)):
        pl.semaphore_signal(bar, inc=1, device_id=dev, device_id_type=MESH)
    pl.semaphore_wait(bar, 9)

    def pp(r):
        return (px, py) if r == 0 else (py, px)

    def nbs(r):
        return ((xn, z), (yn, z)) if r == 0 else ((yn, z), (xn, z))

    def blk(r, p1, p2):
        return pl.ds(pl.multiple_of(384 * r + 96 * (2 * p1 + p2), 32), 96)

    def uof(v):
        return c + v * up

    def w_start(a):
        for v in range(2):
            for r in range(2):
                p1, p2 = pp(r)
                rows = blk(r, p1, p2)
                dst = wg.at[a, uof(v), rows]
                if a > 0:
                    parts = ((zz == v, w_in[a].at[rows]),)
                elif r == 0:
                    parts = ((zz == v, wq_in.at[rows]),)
                else:
                    off = pl.ds(pl.multiple_of(96 * p2, 32), 96)
                    high = pl.ds(pl.multiple_of(384 + 96 * p2, 32), 96)
                    parts = (
                        ((zz == v) & (p1 == 0), wq_in.at[high]),
                        ((zz == v) & (p1 == 1), wo_in.at[off]),
                    )
                near = z + up if v == 0 else z - up
                far = z + 2 * up if v == 0 else z + up
                for cond, src in parts:

                    @pl.when(cond)
                    def _(src=src, dst=dst, v=v, r=r, near=near, far=far):
                        rc(src, dst, wz_s.at[a, v, r], wz_r.at[a, v, r], (d, near)).start()
                        rc(src, dst, wz_s2.at[a, v, r], wz_r.at[a, v, r], (d, far)).start()

    def w_copies(a, v):
        if a > 0:
            return (lc(w_in[a], wg.at[a, uof(v)], w_l.at[a]),)
        return (
            lc(wq_in, wg.at[0, uof(v), pl.ds(0, 576)], w_l.at[0]),
            lc(wo_in, wg.at[0, uof(v), pl.ds(576, 192)], w_l.at[3]),
        )

    def w_local(a):
        for v in range(2):

            @pl.when(zz == v)
            def _(v=v):
                for cp in w_copies(a, v):
                    cp.start()

    def w_fwd(a, stage):
        for v in range(2):
            for r in range(2):
                p1, p2 = pp(r)
                ref = wg.at[a, uof(v), blk(r, p1, p2)]
                n1_, n2_ = nbs(r)
                cond = (zz == 3) if stage else ((zz == 1 - v) | (zz == 2))

                @pl.when(cond)
                def _(ref=ref, v=v, r=r, n1_=n1_, n2_=n2_):
                    wait_recv(ref, wz_r.at[a, v, r])
                    rc(ref, ref, wx_s.at[a, v, r, 0], wx_r.at[a, v, r, 0], n1_).start()
                    rc(ref, ref, wx_s.at[a, v, r, 1], wx_r.at[a, v, r, 1], n2_).start()

                if not stage:

                    @pl.when(zz == 2)
                    def _(ref=ref, v=v, r=r):
                        rc(ref, ref, wz_s.at[a, v, r], wz_r.at[a, v, r], (d, z + up)).start()

    def w_fwd2(a):
        for v in range(2):
            for r in range(2):
                p1, p2 = pp(r)
                ref = wg.at[a, uof(v), blk(r, 1 - p1, p2)]
                n1_, n2_ = nbs(r)

                @pl.when(zz != v)
                def _(ref=ref, v=v, r=r, n2_=n2_):
                    wait_recv(ref, wx_r.at[a, v, r, 0])
                    rc(ref, ref, wx_s.at[a, v, r, 2], wx_r.at[a, v, r, 2], n2_).start()

    def w_done(a):
        for v in range(2):
            for r in range(2):
                p1, p2 = pp(r)

                @pl.when(zz != v)
                def _(v=v, r=r, p1=p1, p2=p2):
                    wait_recv(wg.at[a, uof(v), blk(r, p1, 1 - p2)], wx_r.at[a, v, r, 1])
                    wait_recv(wg.at[a, uof(v), blk(r, 1 - p1, 1 - p2)], wx_r.at[a, v, r, 2])

            @pl.when(zz == v)
            def _(v=v):
                for cp in w_copies(a, v):
                    cp.wait()

    def w_end(a):
        for v in range(2):
            for r in range(2):
                p1, p2 = pp(r)
                ref = wg.at[a, uof(v), blk(r, p1, p2)]

                @pl.when((zz == v) | (zz == 2))
                def _(ref=ref, v=v, r=r):
                    wait_send(ref, wz_s.at[a, v, r])

                @pl.when(zz == v)
                def _(ref=ref, v=v, r=r):
                    wait_send(ref, wz_s2.at[a, v, r])

                @pl.when(zz != v)
                def _(ref=ref, v=v, r=r):
                    for k in range(3):
                        wait_send(ref, wx_s.at[a, v, r, k])

    w_start(0)
    w_local(0)
    lc(x_in, x3, x_l).start()
    for k, ref in enumerate((p0, p1_, p2_, p3_, p4_, p5_)):
        par[k : k + 1, :] = ref[...].astype(F32).reshape(1, 768)
    bias_in[...] = jnp.zeros((8, 768), F32)
    bias_in[0:2, 0:192] = qb_in[...].astype(F32)
    bias_in[2:3, :] = p6_[...].astype(F32).reshape(1, 768)

    for j in range(2):
        dev = (base + zc, 2 * c + j)
        self_ = (zc == c) & (z == 2 * c + j)

        @pl.when(self_)
        def _(j=j):
            lc(ord_in, ordv.at[zj], o_l).start()

        @pl.when(jnp.logical_not(self_))
        def _(j=j, dev=dev):
            rc(ord_in, ordv.at[lax.rem(z, 2)], o_s.at[j], o_r.at[zj], dev).start()

    @pl.when(prim)
    def _():
        for k in range(1, 4):
            dev = (d, lax.rem(z + k, 4))
            rc(bias_in, bias.at[zj], b_s.at[k - 1], b_r.at[zj], dev).start()
        lc(bias_in, bias.at[zj], b_l).start()
        lc(mr_in, mr, m_l.at[0]).start()
        lc(mg_in, mg3, m_l.at[1]).start()
        rc(mr_in, mr, m_s.at[0], m_r.at[0], (sib, z)).start()
        rc(mg_in, mg3, m_s.at[1], m_r.at[1], (sib, z)).start()


    w_local(1)
    w_local(2)
    lc(x_in, x3, x_l).wait()

    def part(k, _):
        both = x3[pl.ds(pl.multiple_of(32 * k, 32), 32)].astype(F32)
        for j in range(2):
            dg[pl.ds(pl.multiple_of(256 * j + 32 * k, 32), 32), 0:768] = both[:, j, :].astype(BF)
        return 0

    lax.fori_loop(0, 8, part, 0)
    w_fwd(0, 0)
    w_fwd(0, 1)

    for j in range(2):
        for h in range(2):
            zt = 2 * c + j
            rows = pl.ds(128 * h, 128)
            self_ = (c == h) & (z == zt)
            src = dg.at[pl.ds(256 * j + 128 * h, 128), 0:768]
            dst = xall.at[pl.ds(pl.multiple_of(256 * z + 128 * h, 128), 128)]

            @pl.when(self_)
            def _(src=src, dst=dst):
                lc(src, dst, x_l).start()

            @pl.when(jnp.logical_not(self_))
            def _(src=src, dst=dst, j=j, h=h, zt=zt):
                rc(src, dst, x_s.at[j, h], x_r.at[z], (base + h, zt)).start()

    w_fwd2(0)

    def xrows(k, h):
        return xall.at[pl.ds(pl.multiple_of(256 * k + 128 * h, 128), 128)]

    for k in range(4):
        ref = xrows(k, c)
        loc = prim & (z == k)

        @pl.when(loc)
        def _(ref=ref):
            lc(ref, ref, x_l).wait()

        @pl.when(jnp.logical_not(loc))
        def _(ref=ref, k=k):
            wait_recv(ref, x_r.at[k])

        rc(ref, ref, cx_s.at[k], cx_r.at[k], (sib, z)).start()
    w_start(1)
    for k in range(4):
        wait_recv(xrows(k, 1 - c), cx_r.at[k])

    for u in range(2):
        loc = prim & (zj == u)

        @pl.when(loc)
        def _(u=u):
            lc(ord_in, ordv.at[u], o_l).wait()
            lc(bias_in, bias.at[u], b_l).wait()

        @pl.when(jnp.logical_not(loc))
        def _(u=u):
            wait_recv(ordv.at[u], o_r.at[u])
            wait_recv(bias.at[u], b_r.at[u])

    @pl.when(prim)
    def _():
        lc(mr_in, mr, m_l.at[0]).wait()
        lc(mg_in, mg3, m_l.at[1]).wait()

    @pl.when(jnp.logical_not(prim))
    def _():
        wait_recv(mr, m_r.at[0])
        wait_recv(mg3, m_r.at[1])

    both = mg3[...].astype(F32)
    mg[...] = jnp.where(zj == 0, both[:, 0, :], both[:, 1, :]).astype(BF)
    w_done(0)

    lane = lax.broadcasted_iota(jnp.int32, (512, 128), 1)
    sub = lax.broadcasted_iota(jnp.int32, (512, 1024), 0)
    low = lane < 64

    def place(h, kind):
        return h // 3, slice(192 * kind + 64 * (h % 3), 192 * kind + 64 * (h % 3) + 64)

    def pair_rows(i):
        a, b = 2 * i, 2 * i + 1
        return (place(a, 1), place(a, 2), place(a, 0), place(b, 0), place(b, 2), place(b, 1))

    for i in range(3):
        for n, (u, rows) in enumerate(pair_rows(i)):
            wq[384 * i + 64 * n : 384 * i + 64 * n + 64, :] = wg[0, u, rows, :]
        for n, (u, rows) in enumerate((place(2 * i + 1, 3), place(2 * i, 3))):
            wo[128 * i + 64 * n : 128 * i + 64 * n + 64, :] = wg[0, u, rows, :]

    def bq(i):
        nil = jnp.zeros((1, 64), F32)

        def take(h, row):
            return bias[h // 3, row : row + 1, 64 * (h % 3) : 64 * (h % 3) + 64]

        a, b = 2 * i, 2 * i + 1
        return jnp.concatenate(
            [nil, take(a, 1), take(a, 0), take(b, 0), take(b, 1), nil], axis=1
        )

    def rows_of(m, n):
        return pl.ds(pl.multiple_of(m * n, n), n)

    for lo_, hi_ in ((0, 2), (2, 3)):
        bv = jnp.concatenate([bq(i) for i in range(lo_, hi_)], axis=1)
        cols = slice(384 * lo_, 384 * hi_)

        def body(k, _, cols=cols, bv=bv):
            rr = rows_of(k, 512)
            qkv[rr, cols] = (mm(xall[rr, :], wq[cols, :], NT) + bv).astype(BF)
            return 0

        lax.fori_loop(0, 2, body, 0)

    w_start(2)

    def columns(h, s):
        row = ordv[h // 3, h % 3, pl.ds(zj, 1), :]
        oc[s] = jnp.broadcast_to(row, (128, 1024)).T

    def sort_mat(s, t):
        b = oc[s, rows_of(t, 512), :]
        return jnp.concatenate(
            [jnp.where(b == lane + 128 * k, 1.0, 0.0).astype(BF) for k in range(8)], axis=1
        )

    def unsort_mat(h, t):
        row = ordv[h // 3, h % 3, pl.ds(zj, 1), :]
        return jnp.where(sub + 512 * t == row, 1.0, 0.0).astype(BF)

    four = range(4)

    def piece(w, k):
        return w[128 * k : 128 * k + 128]

    def attend(i):
        for s in range(2):
            columns(2 * i + s, s)

        def body(t, _):
            rr = rows_of(t, 512)
            q, kv = [], []
            for s in range(2):
                at_ = 384 * i + 128 * s
                w = mm(sort_mat(s, t), qkv[:, at_ : at_ + 256])
                if s == 0:
                    kv.append(w[:, 0:128].astype(BF))
                    q.append((jnp.where(low, w[:, 128:256], 0.0) * 0.125).astype(BF))
                else:
                    q.append((jnp.where(low, 0.0, w[:, 0:128]) * 0.125).astype(BF))
                    kv.append(w[:, 128:256].astype(BF))
                sq[2 * i + s, rr, :] = q[s]
                skv[2 * i + s, rr, :] = kv[s]
            for s in range(2):
                sc = [mm(piece(q[s], k), piece(kv[s], k), NT) for k in four]
                sc = jnp.concatenate(sc, axis=0)
                ex = jnp.exp(sc - jnp.max(sc, axis=-1, keepdims=True))
                prob = ex * (1.0 / jnp.sum(ex, axis=-1, keepdims=True))
                pr[2 * i + s, rr, :] = prob
                pb = prob.astype(BF)
                mx = jnp.concatenate([mm(piece(pb, k), piece(kv[s], k)) for k in four], axis=0)
                keep = jnp.where(low, 0.0, mx) if s == 0 else jnp.where(low, mx, 0.0)
                ms[s][rr, 0:128] = keep.astype(BF)
            return 0

        lax.fori_loop(0, 2, body, 0)

        def back(t, _):
            both = mm(unsort_mat(2 * i, t), ms[0][:, 0:128]) + mm(
                unsort_mat(2 * i + 1, t), ms[1][:, 0:128]
            )
            mix[rows_of(t, 512), 128 * i : 128 * i + 128] = both.astype(BF)
            return 0

        lax.fori_loop(0, 2, back, 0)

    attend(0)
    w_fwd(1, 0)
    attend(1)
    w_fwd(1, 1)
    w_fwd2(1)
    attend(2)
    w_fwd(2, 0)

    mine = 512 * c
    other = 512 - mine

    def at(off, m, n):
        return pl.ds(pl.multiple_of(off + m * n, n), n)

    def partial(fn, k):
        if k >= 2:
            wait_send(snd.at[k % 2], pe_s.at[k - 2])
        for n in range(3):
            cols = slice(256 * n, 256 * n + 256)
            snd[k % 2, :, cols] = fn(at(other, 0, 512), cols).astype(BF)
        rc(snd.at[k % 2], rcv.at[k], pe_s.at[k], pe_r.at[k], (sib, z)).start()
        for n in range(3):
            cols = slice(256 * n, 256 * n + 256)
            op[:, cols] = fn(at(mine, 0, 512), cols)
        wait_recv(rcv.at[k], pe_r.at[k])

    def share(ref, k):
        own = ref.at[pl.ds(pl.multiple_of(mine, 512), 512)]
        rc(own, own, pe_s.at[4 + k], pe_r.at[4 + k], (sib, z)).start()

    def shared(ref, k):
        wait_recv(ref.at[pl.ds(pl.multiple_of(other, 512), 512)], pe_r.at[4 + k])

    partial(lambda rows, cols: mm(mix[rows, :], wo[:, cols]), 0)

    def norm1(m, _):
        rr = rows_of(m, 128)
        v = (
            xall[at(mine, m, 128), :].astype(F32)
            + op[rr, :]
            + rcv[0, rr, :].astype(F32)
            + par[0:1, :]
        )
        cen = v - jnp.mean(v, axis=-1, keepdims=True)
        rstd = lax.rsqrt(jnp.mean(cen * cen, axis=-1, keepdims=True) + NORM_EPS)
        nv = cen * rstd
        n1[rr, :] = nv
        rs1[rr, :] = rstd
        fv = nv * par[1:2, :] + par[2:3, :]
        fst[rr, :] = fv
        flow[at(mine, m, 128), :] = fv.astype(BF)
        return 0

    lax.fori_loop(0, 4, norm1, 0)
    share(flow, 0)
    w_fwd(2, 1)
    w_done(1)

    for j in range(2):
        for h in range(2):

            @pl.when(jnp.logical_not((c == h) & (z == 2 * c + j)))
            def _(j=j, h=h):
                wait_send(dg.at[pl.ds(0, 128), 0:768], x_s.at[j, h])

    def hidden(t):
        return lax.div(t, 3), rows_of(lax.rem(t, 3), 256)

    def ffn_up(off):
        def body(t, _):
            u, cols = hidden(t)
            rr = at(off, 0, 512)
            h = mm(flow[rr, :], wg[1, u, :, cols]) + bias[u, 2:3, cols]
            cdf = 0.5 + 0.5 * lax.erf(h * RSQRT2)
            act[rr, rows_of(t, 256)] = (h * cdf).astype(BF)
            dg[rr, rows_of(t, 256)] = (cdf + h * (jnp.exp(-0.5 * h * h) * RSQRT2PI)).astype(BF)
            return 0

        lax.fori_loop(0, 6, body, 0)

    ffn_up(mine)
    w_fwd2(2)
    shared(flow, 0)
    ffn_up(other)
    w_done(2)
    partial(
        lambda rows, cols: mm(act[rows, 0:768], wg[2, 0, :, cols])
        + mm(act[rows, 768:1536], wg[2, 1, :, cols]),
        1,
    )

    w_end(0)

    vb[0] = jnp.zeros((16, 768), F32)
    ones8 = jnp.zeros((1, 768), F32)

    def norm2(m, carry):
        sgain, sshift, dbias = carry
        rr = rows_of(m, 128)
        v = fst[rr, :] + op[rr, :] + rcv[1, rr, :].astype(F32) + par[3:4, :]
        cen = v - jnp.mean(v, axis=-1, keepdims=True)
        rstd = lax.rsqrt(jnp.mean(cen * cen, axis=-1, keepdims=True) + NORM_EPS)
        nv = cen * rstd
        tok[rr, :] = (nv * par[4:5, :] + par[5:6, :]).astype(BF)
        pos = lax.broadcasted_iota(jnp.int32, (128, mr.shape[1]), 0) + (mine + 128 * m)
        hits = jnp.where(pos == mr[pl.ds(zj, 1), :], 1.0, 0.0).astype(BF)
        dout = mm(hits, mg[...])
        gg = dout * par[4:5, :]
        d2 = (
            gg
            - jnp.mean(gg, axis=-1, keepdims=True)
            - nv * jnp.mean(gg * nv, axis=-1, keepdims=True)
        ) * rstd
        fst[rr, :] = d2
        dlo = d2.astype(BF)
        dl[at(mine, m, 128), :] = dlo
        return (
            sgain + jnp.sum(dout * nv, axis=0, keepdims=True),
            sshift + jnp.sum(dout, axis=0, keepdims=True),
            dbias + jnp.sum(dlo.astype(F32), axis=0, keepdims=True),
        )

    sg, ss, db = lax.fori_loop(0, 4, norm2, (ones8, ones8, ones8))
    share(dl, 1)
    vb[0, 0:1, :] = sg
    vb[0, 1:2, :] = ss
    vb[0, 2:3, :] = db

    def tok_send(src, dst, k):
        for u in range(2):
            self_ = prim & (z == 2 * c + u)
            s_ = src.at[pl.ds(256 * u, 256)]
            d_ = dst.at[zj]

            @pl.when(self_)
            def _(s_=s_, d_=d_):
                lc(s_, d_, t_l.at[k]).start()

            @pl.when(jnp.logical_not(self_))
            def _(s_=s_, d_=d_, u=u):
                rc(s_, d_, t_s.at[k, u], t_r.at[k, zj], (base + zc, 2 * c + u)).start()

    def tok_wait(src, dst, k):
        for j in range(2):
            loc = prim & (z == 2 * c + j)

            @pl.when(loc)
            def _(j=j):
                lc(src.at[pl.ds(0, 256)], dst.at[j], t_l.at[k]).wait()

            @pl.when(jnp.logical_not(loc))
            def _(j=j):
                wait_recv(dst.at[j], t_r.at[k, j])
                wait_send(src.at[pl.ds(0, 256)], t_s.at[k, j])

    tok_send(tok, o1, 0)

    def g_start(a, u):
        for r in range(2):
            p1, p2 = pp(r)
            src = g.at[a, u, pl.ds(pl.multiple_of(384 * r + 192 * (1 - p1), 64), 192)]
            rc(src, st1.at[a, u, r], g1_s.at[a, u, r], g1_r.at[a, u, r], nbs(r)[0]).start()

    def quarter(ref, r, q):
        return ref.at[pl.ds(pl.multiple_of(96 * q, 32), 96)]

    def g_step2(a, u):
        for r in range(2):
            p1, p2 = pp(r)
            wait_recv(st1.at[a, u, r], g1_r.at[a, u, r])
            rows = blk(r, p1, 1 - p2)
            part = st1[a, u, r, pl.ds(pl.multiple_of(96 * (1 - p2), 32), 96), :]
            g[a, u, rows, :] = (g[a, u, rows, :].astype(F32) + part.astype(F32)).astype(BF)
            rc(
                g.at[a, u, rows], st2.at[a, u, r], g2_s.at[a, u, r], g2_r.at[a, u, r], nbs(r)[1]
            ).start()

    def g_step3(a, u):
        for r in range(2):
            p1, p2 = pp(r)
            wait_recv(st2.at[a, u, r], g2_r.at[a, u, r])
            rows = blk(r, p1, p2)
            part = st1[a, u, r, pl.ds(pl.multiple_of(96 * p2, 32), 96), :]
            tot = (
                g[a, u, rows, :].astype(F32) + part.astype(F32) + st2[a, u, r].astype(F32)
            ).astype(BF)
            self_ = (c == r) & (z == 2 * c + u)

            @pl.when(self_)
            def _(tot=tot):
                st3[a, z] = tot

            @pl.when(jnp.logical_not(self_))
            def _(tot=tot, rows=rows, r=r):
                g[a, u, rows, :] = tot
                rc(
                    g.at[a, u, rows], st3.at[a, z], g3_s.at[a, u, r], g3_r.at[a, z],
                    (base + r, 2 * c + u),
                ).start()

    q1 = px + c * (py - px)
    q2 = py + c * (px - py)
    e1 = (xn + c * (yn - xn), z)
    e2 = (yn + c * (xn - yn), z)

    def own(r, p1, p2):
        return pl.ds(pl.multiple_of(384 * r + 96 * (2 * p1 + p2), 32), 96)

    def g_step4(a):
        for k in range(4):
            loc = prim & (z == k)

            @pl.when(jnp.logical_not(loc))
            def _(k=k):
                wait_recv(st3.at[a, k], g3_r.at[a, k])

        rb[a] = (
            st3[a, 0].astype(F32)
            + st3[a, 1].astype(F32)
            + st3[a, 2].astype(F32)
            + st3[a, 3].astype(F32)
        ).astype(BF)
        dst = res[a].at[own(c, q1, q2)]
        rc(rb.at[a], dst, ag_s.at[a, 0], ag_r.at[a, 0], e1).start()
        rc(rb.at[a], dst, ag_s.at[a, 1], ag_r.at[a, 1], e2).start()
        rc(rb.at[a], dst, ce_s.at[a, 0], ce_r.at[a, 0], (sib, z)).start()
        lc(rb.at[a], dst, ag_l.at[a]).start()

    def g_step5(a):
        ref = res[a].at[own(c, 1 - q1, q2)]
        wait_recv(ref, ag_r.at[a, 0])
        rc(ref, ref, ag_s.at[a, 2], ag_r.at[a, 2], e2).start()
        rc(ref, ref, ce_s.at[a, 1], ce_r.at[a, 1], (sib, z)).start()

    def g_step6(a):
        ref = res[a].at[own(c, q1, 1 - q2)]
        wait_recv(ref, ag_r.at[a, 1])
        rc(ref, ref, ce_s.at[a, 2], ce_r.at[a, 2], (sib, z)).start()
        ref = res[a].at[own(c, 1 - q1, 1 - q2)]
        wait_recv(ref, ag_r.at[a, 2])
        rc(ref, ref, ce_s.at[a, 3], ce_r.at[a, 3], (sib, z)).start()

    def g_end(a):
        lc(rb.at[a], res[a].at[own(c, q1, q2)], ag_l.at[a]).wait()
        o_ = 1 - c
        for k, rows in enumerate(
            (own(o_, q2, q1), own(o_, 1 - q2, q1), own(o_, q2, 1 - q1), own(o_, 1 - q2, 1 - q1))
        ):
            wait_recv(res[a].at[rows], ce_r.at[a, k])
            wait_send(rb.at[a], ce_s.at[a, k])
        for k in range(3):
            wait_send(rb.at[a], ag_s.at[a, k])
        for u in range(2):
            for r in range(2):
                wait_send(st1.at[a, u, r], g1_s.at[a, u, r])
                wait_send(st2.at[a, u, r], g2_s.at[a, u, r])

                @pl.when(jnp.logical_not((c == r) & (z == 2 * c + u)))
                def _(u=u, r=r):
                    wait_send(st2.at[a, u, r], g3_s.at[a, u, r])

    shared(dl, 1)

    for u in range(2):
        for n in range(3):
            cols = slice(768 * u + 256 * n, 768 * u + 256 * n + 256)
            g[2, u, 256 * n : 256 * n + 256, :] = mm(act[:, cols], dl[...], TN).astype(BF)
        g_start(2, u)

    def dup(t, _):
        u, cols = hidden(t)
        ub = jnp.zeros((1, 256), F32)
        for m in range(2):
            rr = slice(512 * m, 512 * m + 512)
            dv = mm(dl[rr, :], wg[2, u, cols, :], NT) * dg[rr, rows_of(t, 256)].astype(F32)
            dv = dv.astype(BF)
            dg[rr, rows_of(t, 256)] = dv
            ub = ub + jnp.sum(dv.astype(F32), axis=0, keepdims=True)
        vb[0, pl.ds(6 + 2 * c + u, 1), cols] = ub
        return 0

    lax.fori_loop(0, 6, dup, 0)
    partial(
        lambda rows, cols: mm(dg[rows, 0:768], wg[1, 0, cols, :], NT)
        + mm(dg[rows, 768:1536], wg[1, 1, cols, :], NT),
        2,
    )
    for u in range(2):
        for n in range(3):
            g[1, u, 256 * n : 256 * n + 256, :] = mm(
                flow[:, 256 * n : 256 * n + 256], dg[:, 768 * u : 768 * u + 768], TN
            ).astype(BF)
        g_start(1, u)

    wait_send(dl.at[pl.ds(0, 512)], pe_s.at[5])
    def norm1b(m, carry):
        fg, fs, ob = carry
        rr = rows_of(m, 128)
        df = fst[rr, :] + op[rr, :] + rcv[2, rr, :].astype(F32)
        nv = n1[rr, :]
        gg = df * par[1:2, :]
        dr = (
            gg
            - jnp.mean(gg, axis=-1, keepdims=True)
            - nv * jnp.mean(gg * nv, axis=-1, keepdims=True)
        ) * rs1[rr, :]
        fst[rr, :] = dr
        dlo = dr.astype(BF)
        dl[at(mine, m, 128), :] = dlo
        return (
            fg + jnp.sum(df * nv, axis=0, keepdims=True),
            fs + jnp.sum(df, axis=0, keepdims=True),
            ob + jnp.sum(dlo.astype(F32), axis=0, keepdims=True),
        )

    fg, fs, ob = lax.fori_loop(0, 4, norm1b, (ones8, ones8, ones8))
    share(dl, 2)
    vb[0, 3:4, :] = fg
    vb[0, 4:5, :] = fs
    vb[0, 5:6, :] = ob
    shared(dl, 2)
    for u in range(2):
        g_step2(2, u)

    def dmix(m, _):
        rr = rows_of(m, 512)
        dm[rr, :] = mm(dl[rr, :], wo[...], NT).astype(BF)
        return 0

    lax.fori_loop(0, 2, dmix, 0)
    for i in range(3):
        gw = mm(mix[:, 128 * i : 128 * i + 128], dl[...], TN).astype(BF)
        for n, (u, rows) in enumerate((place(2 * i + 1, 3), place(2 * i, 3))):
            g[0, u, rows, :] = gw[64 * n : 64 * n + 64, :]

    def attend_back(i):
        for s in range(2):
            columns(2 * i + s, s)

        def body(t, _):
            rr = rows_of(t, 512)
            uu = []
            for s in range(2):
                w = mm(sort_mat(s, t), dm[:, 128 * i : 128 * i + 128])
                uu.append(
                    (jnp.where(low, 0.0, w) if s == 0 else jnp.where(low, w, 0.0)).astype(BF)
                )
            for s in range(2):
                kv = skv[2 * i + s, rr, :]
                q = sq[2 * i + s, rr, :]
                prob = pr[2 * i + s, rr, :]
                dp = jnp.concatenate(
                    [mm(piece(uu[s], k), piece(kv, k), NT) for k in four], axis=0
                )
                cen = jnp.sum(prob * dp, axis=-1, keepdims=True)
                ds = (prob * (dp - cen)).astype(BF)
                dq = jnp.concatenate([mm(piece(ds, k), piece(kv, k)) for k in four], axis=0) * 0.125
                pb = prob.astype(BF)
                dkv = jnp.concatenate(
                    [
                        mm(
                            jnp.concatenate([piece(pb, k), piece(ds, k)], axis=0),
                            jnp.concatenate([piece(uu[s], k), piece(q, k)], axis=0),
                            TN,
                        )
                        for k in four
                    ],
                    axis=0,
                ).astype(BF)
                if s == 0:
                    ms[s][rr, 0:128] = dkv
                    ms[s][rr, 128:256] = jnp.where(low, dq, 0.0).astype(BF)
                else:
                    ms[s][rr, 0:128] = jnp.where(low, 0.0, dq).astype(BF)
                    ms[s][rr, 128:256] = dkv
            return 0

        lax.fori_loop(0, 2, body, 0)

        def back(t, carry):
            ga = mm(unsort_mat(2 * i, t), ms[0][...])
            gb = mm(unsort_mat(2 * i + 1, t), ms[1][...])
            out = jnp.concatenate(
                [ga[:, 0:128], ga[:, 128:256] + gb[:, 0:128], gb[:, 128:256]], axis=1
            )
            qkv[rows_of(t, 512), 384 * i : 384 * i + 384] = out.astype(BF)
            return carry + jnp.sum(out, axis=0, keepdims=True)

        return lax.fori_loop(0, 2, back, jnp.zeros((1, 384), F32))

    def gqkv(i):
        gw = mm(qkv[:, 384 * i : 384 * i + 384], xall[...], TN).astype(BF)
        for k, (u, rows) in enumerate(pair_rows(i)):
            g[0, u, rows, :] = gw[64 * k : 64 * k + 64, :]

    b0 = attend_back(0)
    gqkv(0)
    for u in range(2):
        g_step3(2, u)
    b1 = attend_back(1)
    gqkv(1)
    g_start(0, 0)
    for u in range(2):
        g_step2(1, u)
    b2 = attend_back(2)
    gqkv(2)
    g_start(0, 1)
    for u in range(2):
        g_step3(1, u)
    g_step4(2)
    bs = (b0, b1, b2)
    rest = jnp.zeros((1, 384), F32)
    for u in range(2):
        heads = range(3 * u, 3 * u + 3)
        qs = [bs[h // 2][:, 128 + 64 * (h % 2) : 192 + 64 * (h % 2)] for h in heads]
        vs = [bs[h // 2][:, 64 + 192 * (h % 2) : 128 + 192 * (h % 2)] for h in heads]
        vb[0, pl.ds(10 + 2 * c + u, 1), :] = jnp.concatenate(qs + vs + [rest], axis=1)

    vdev = (
        (sib, z), (xn, z), (yn, z), (d, z + 1 - 2 * zj), (d, z + 2 - 4 * zc),
    )

    def v_send(k):
        rc(vb.at[k], vr.at[k], v_s.at[k], v_r.at[k], vdev[k]).start()

    def v_add(k):
        wait_recv(vr.at[k], v_r.at[k])
        vb[k + 1] = vb[k] + vr[k]

    v_send(0)
    partial(
        lambda rows, cols: mm(qkv[rows, :], wq[:, cols]),
        3,
    )

    def gin(m, _):
        rr = rows_of(m, 128)
        gtok[rr, :] = (fst[rr, :] + op[rr, :] + rcv[3, rr, :].astype(F32)).astype(BF)
        return 0

    lax.fori_loop(0, 4, gin, 0)
    tok_send(gtok, o2, 1)
    v_add(0)
    v_send(1)
    g_step2(0, 0)
    g_step5(2)
    g_step3(0, 0)
    v_add(1)
    v_send(2)
    g_step2(0, 1)
    g_step6(2)
    g_step4(1)
    v_add(2)
    v_send(3)
    g_step3(0, 1)
    g_step5(1)
    v_add(3)
    v_send(4)
    g_step6(1)
    g_step4(0)
    g_step5(0)
    v_add(4)
    vout[...] = vb[5]
    vout[14:15, :] = vb[5, pl.ds(6 + z, 1), :]
    vout[15:16, :] = vb[5, pl.ds(10 + z, 1), :]
    g_step6(0)
    for a in range(3):
        g_end(a)
    tok_wait(tok, o1, 0)
    tok_wait(gtok, o2, 1)

    for a in range(1, 3):
        w_end(a)
    for k in range(4):
        wait_send(xrows(k, c), cx_s.at[k])
        if k >= 2:
            wait_send(rcv.at[k], pe_s.at[k])
    for k in (0, 2):
        wait_send(flow.at[pl.ds(0, 512)], pe_s.at[4 + k])
    for k in range(5):
        wait_send(vb.at[k], v_s.at[k])
    for j in range(2):

        @pl.when(jnp.logical_not(prim & (z == 2 * c + j)))
        def _(j=j):
            wait_send(ord_in, o_s.at[j])

    @pl.when(prim)
    def _():
        for k in range(3):
            wait_send(bias_in, b_s.at[k])
        wait_send(mr_in, m_s.at[0])
        wait_send(mg_in, m_s.at[1])


def layer(x, order, wqkv, wout, wb, wc, mr, mg, *small):
    dma = pltpu.SemaphoreType.DMA
    hbm = pl.BlockSpec(memory_space=pl.ANY)
    vmem = pl.BlockSpec(memory_space=pltpu.VMEM)
    V = pltpu.VMEM
    return pl.pallas_call(
        kernel,
        out_shape=(
            jax.ShapeDtypeStruct((2, 256, 768), BF),
            jax.ShapeDtypeStruct((2, 256, 768), BF),
            jax.ShapeDtypeStruct((768, 768), BF),
            jax.ShapeDtypeStruct((768, 768), BF),
            jax.ShapeDtypeStruct((768, 768), BF),
            jax.ShapeDtypeStruct((16, 768), F32),
        ),
        in_specs=[hbm] * 8 + [vmem] * 8,
        out_specs=(hbm, hbm, hbm, hbm, hbm, vmem),
        scratch_shapes=[
            V((1024, 768), BF),
            V((256, 2, 768), BF),
            V((2, 3, 2, 1024), jnp.int32),
            V((3, 2, 768, 768), BF),
            V((2, 8, 768), F32),
            V((8, 768), F32),
            V((8, 768), F32),
            V(mr.shape, jnp.int32),
            V(mg.shape, BF),
            V((mg.shape[0], 768), BF),
            V((1152, 768), BF),
            V((384, 768), BF),
            V((1024, 1152), BF),
            V((2, 1024, 128), jnp.int32),
            V((6, 1024, 128), BF),
            V((6, 1024, 128), BF),
            V((6, 1024, 128), F32),
            V((1024, 384), BF),
            V((2, 512, 768), BF),
            V((4, 512, 768), BF),
            V((512, 768), F32),
            V((512, 768), F32),
            V((512, 768), F32),
            V((512, 1), F32),
            V((1024, 768), BF),
            V((1024, 1536), BF),
            V((1024, 1536), BF),
            V((1024, 768), BF),
            V((3, 2, 768, 768), BF),
            V((3, 2, 2, 192, 768), BF),
            V((3, 2, 2, 96, 768), BF),
            V((3, 4, 96, 768), BF),
            V((3, 96, 768), BF),
            V((6, 16, 768), F32),
            V((5, 16, 768), F32),
            dma((2, 2)), dma((4,)), dma, dma((4,)), dma((4,)),
            dma((2,)), dma((2,)), dma,
            dma((3,)), dma((2,)), dma,
            dma((2,)), dma((2,)), dma((2,)),
            dma((3, 2, 2)), dma((3, 2, 2)), dma((3, 2, 2)),
            dma((3, 2, 2, 3)), dma((3, 2, 2, 3)), dma((4,)),
            dma((7,)), dma((7,)),
            dma((2, 2)), dma((2, 2)), dma((2,)),
            dma((5,)), dma((5,)),
            dma((3, 2, 2)), dma((3, 2, 2)), dma((3, 2, 2)), dma((3, 2, 2)),
            dma((3, 2, 2)), dma((3, 4)), dma((3, 3)), dma((3, 3)), dma((3,)),
            dma((3, 4)), dma((3, 4)),
        ],
        compiler_params=pltpu.CompilerParams(
            collective_id=0, has_side_effects=True, vmem_limit_bytes=60 * 2**20
        ),
    )(x, order, wqkv, wout, wb, wc, mr, mg, *small)


def finish_kernel(
    o1, o2, ra, rb, rc, vec, out, gin, gq, go, gb, gc, fg, fs, ob, db, sg, ss, ub, qv,
    o1v, o2v, rv, outv, ginv, gv, in_sem, out_sem,
):
    loads = [
        pltpu.make_async_copy(a, b, in_sem.at[k])
        for k, (a, b) in enumerate(
            ((o1, o1v), (o2, o2v), (ra, rv.at[0]), (rb, rv.at[1]), (rc, rv.at[2]))
        )
    ]
    for k in (2, 3, 4, 1, 0):
        loads[k].start()
    stores = [
        pltpu.make_async_copy(a, b, out_sem.at[k])
        for k, (a, b) in enumerate(
            (
                (gv.at[0, pl.ds(0, 576)], gq), (gv.at[0, pl.ds(576, 192)], go),
                (gv.at[1], gb), (gv.at[2], gc), (ginv, gin), (outv, out),
            )
        )
    ]
    for ref, row in ((sg, 0), (ss, 1), (db, 2), (fg, 3), (fs, 4), (ob, 5), (ub, 14)):
        ref[...] = vec[row, :]
    wide = qv.shape[1]
    qv[0:1, :] = vec[15:16, 0:wide]
    qv[1:2, :] = vec[15:16, wide : 2 * wide]

    for a in range(3):
        loads[2 + a].wait()

        def body(k, _, a=a):
            rr = pl.ds(pl.multiple_of(k * 96, 96), 96)
            gv[a, rr, :] = rv[a, rr, :].astype(F32)
            return 0

        lax.fori_loop(0, 8, body, 0)
        if a == 0:
            stores[0].start()
            stores[1].start()
        else:
            stores[a + 1].start()

    def weave(src, dst, dtype):
        def body(k, _):
            rr = pl.ds(pl.multiple_of(k * 32, 32), 32)
            both = jnp.stack([src[0, rr, :].astype(F32), src[1, rr, :].astype(F32)], axis=1)
            dst[rr] = both.astype(dtype)
            return 0

        lax.fori_loop(0, 8, body, 0)

    loads[1].wait()
    weave(o2v, ginv, F32)
    stores[4].start()
    loads[0].wait()
    weave(o1v, outv, BF)
    stores[5].start()
    for cp in stores:
        cp.wait()


def finish(o1, o2, ra, rb, rc, vec):
    hbm = pl.BlockSpec(memory_space=pl.ANY)
    vmem = pl.BlockSpec(memory_space=pltpu.VMEM)
    V = pltpu.VMEM
    S = jax.ShapeDtypeStruct
    row = S((768,), F32)
    return pl.pallas_call(
        finish_kernel,
        out_shape=(
            S((256, 2, 768), BF), S((256, 2, 768), F32), S((576, 768), F32), S((192, 768), F32),
            S((768, 768), F32), S((768, 768), F32), row, row, row, row, row, row, row,
            S((2, 192), F32),
        ),
        in_specs=[hbm] * 5 + [vmem],
        out_specs=(hbm,) * 6 + (vmem,) * 8,
        scratch_shapes=[
            V((2, 256, 768), BF), V((2, 256, 768), BF), V((3, 768, 768), BF),
            V((256, 2, 768), BF), V((256, 2, 768), F32), V((3, 768, 768), F32),
            pltpu.SemaphoreType.DMA((5,)), pltpu.SemaphoreType.DMA((6,)),
        ],
        compiler_params=pltpu.CompilerParams(vmem_limit_bytes=60 * 2**20),
    )(o1, o2, ra, rb, rc, vec)


def shards(
    inputs, qkv_weight, qv_bias, out_weight, out_bias, first_gain, first_shift,
    first_layer_weight, first_layer_bias, second_layer_weight, second_layer_bias,
    second_gain, second_shift, cluster_order, masked_rows, masked_grad,
):
    t = lax.axis_index("tensor")
    heads = qkv_weight.shape[2]
    wqkv = qkv_weight.transpose(1, 2, 0).reshape(3 * heads, 768)
    order = cluster_order.transpose(1, 0, 2)

    o1, o2, ra, rb, rc, vec = layer(
        inputs, order, wqkv, out_weight, first_layer_weight, second_layer_weight,
        masked_rows, masked_grad.transpose(1, 0, 2), qv_bias,
        out_bias, first_gain, first_shift, second_layer_bias, second_gain, second_shift,
        first_layer_bias,
    )

    many = lax.axis_size("dp") // 8
    if many > 1:
        groups = [[8 * i + j for i in range(many)] for j in range(8)]
        ra, rb, rc = lax.psum(
            (ra.astype(F32), rb.astype(F32), rc.astype(F32)), "dp", axis_index_groups=groups
        )
        ra, rb, rc = ra.astype(BF), rb.astype(BF), rc.astype(BF)
        vec = lax.psum(vec, "dp", axis_index_groups=groups)
    outputs, grad_inputs, gq, go, gb, gc, fg, fs, ob, db, sg, ss, ub, qv = finish(
        o1, o2, ra, rb, rc, vec
    )
    return (
        outputs,
        grad_inputs,
        gq.reshape(3, heads, 768).transpose(2, 0, 1),
        qv,
        go,
        ob,
        fg,
        fs,
        gb,
        ub,
        gc,
        db,
        sg,
        ss,
    )


def solution(mesh):
    placed = (
        P("tensor", "dp", None), P(None, None, "tensor"), P(None, "tensor"), P("tensor", None),
        P(), P(), P(), P(None, "tensor"), P("tensor"), P("tensor", None), P(), P(), P(),
        P("dp", "tensor", None), P("dp", None), P("dp", None, None),
    )
    return jax.shard_map(
        shards,
        mesh=mesh,
        in_specs=placed,
        out_specs=(
            P("tensor", "dp", None), P("tensor", "dp", None), P(None, None, "tensor"),
            P(None, "tensor"), P("tensor", None), P(), P(), P(), P(None, "tensor"), P("tensor"),
            P("tensor", None), P(), P(), P(),
        ),
        check_vma=False,
    )
```

time: 309 us -> 205 us (0.66)
  Pallas kernels: 258 us -> 204 us
  local copies, waits for them, and re-layouts: 38 us -> 0 us
  other arithmetic: 8.24 us -> 0 us
    pallas_call x1, Pallas kernels: 258 us -> 197 us  [layer(): pl.pallas_call(kernel, out_shape=(jax.ShapeDtypeStruct((2, 256, 768), BF)...]
    slice x15 -> x0, local copies, waits for them, and re-layouts: 13.1 us -> none  [the longest x10 5.87 us: split64(): return [a[..., 64 * k:64 * k + 64] for k in range(n)]]
    concatenate x10 -> x0, local copies, waits for them, and re-layouts: 11.8 us -> none  [the longest x2 3.76 us: restore(): jnp.concatenate(od, axis=-1)]
    unnamed x40 -> x0, local copies, waits for them, and re-layouts: 7.93 us -> none
    pallas_call x0 -> x1, Pallas kernels: none -> 7.15 us  [finish(): pl.pallas_call(finish_kernel, out_shape=(S((256, 2, 768), BF), S((256, 2,...]
    convert_element_type x3 -> x0, other arithmetic: 4.52 us -> none  [the longest x1 2.59 us: shards(): res = res.astype(F32)]
    select_n x4 -> x0, other arithmetic: 3.12 us -> none  [the longest x2 1.97 us: restore(): jnp.where(even, jnp.concatenate(ev, axis=-1), jnp.concatenate(od, axis=-1))]
where the time goes in v2:
time: 205 us
  Pallas kernels  204 us (100%)
    pallas_call x1, Pallas kernels, layer(): pl.pallas_call(kernel, out_shape=(jax.ShapeDtypeStruct((2, 256, 768), BF)...  197 us
    pallas_call x1, Pallas kernels, finish(): pl.pallas_call(finish_kernel, out_shape=(S((256, 2, 768), BF), S((256, 2,...  7.15 us

profile of v2, /device:TPU:9, one launch (start us, length us, event | category | flops | bytes accessed | tf_op | source)
XLA Modules:
  0.0 204.6 jit_solution(11593869042906665398)
XLA Ops:
  0.7 196.6 %shard_map.263 = (bf16[2,256,768]{2,1,0:T(8,128)(2,1)}, bf16[2,256,768]{2,1,0:T(8,128)(2,1)}, bf16[768,768]{1,0:T(8,128)(2,1)}, bf16[768,768]{1,0:T(8,128)(2,1)}...) custom-call(bf16[256,2,768]{2,1,0:T(2,128)(2,1)} %x_in.1, s32[3,2,1024]{2,1,0:T(2,128)} %bitcast.10, ...), custom_call_target="tpu_custom_call" | custom-call | tf_op jit(solution)/shard_map/pallas_call | solution.py:920
  197.3 7.1 %shard_map.264 = (bf16[256,2,768]{2,1,0:T(2,128)(2,1)}, f32[256,2,768]{2,1,0:T(2,128)}, f32[576,768]{1,0:T(8,128)}, f32[192,768]{1,0:T(8,128)}, f32[768,768]{1,0...) custom-call(bf16[2,256,768]{2,1,0:T(8,128)(2,1)} %get-tuple-element., ...), custom_call_target="tpu_custom_call" | custom-call | tf_op jit(solution)/shard_map/pallas_call | solution.py:1054

commit v3 on v2

--- a/solution.py
+++ b/solution.py
@@ -13,6 +13,7 @@
 BF = jnp.bfloat16
 F32 = jnp.float32
 MESH = pl.DeviceIdType.MESH
+DIRECT = (2,)
 RSQRT2 = 1.0 / math.sqrt(2.0)
 RSQRT2PI = 1.0 / math.sqrt(2.0 * math.pi)
 
@@ -33,7 +34,7 @@
     snd, rcv, op, fst, n1, rs1, flow, act, dg, dl, g, st1, st2, st3,
     rb, vb, vr,
     x_s, x_r, x_l, cx_s, cx_r, o_s, o_r, o_l, b_s, b_r, b_l, m_s, m_r, m_l,
-    wz_s, wz_s2, wz_r, wx_s, wx_r, w_l, pe_s, pe_r, t_s, t_r, t_l, v_s, v_r,
+    wz_s, wz_s2, wz_s3, wz_r, wx_s, wx_r, w_l, pe_s, pe_r, t_s, t_r, t_l, v_s, v_r,
     g1_s, g1_r, g2_s, g2_r, g3_s, g3_r, ag_s, ag_r, ag_l, ce_s, ce_r,
 ):
     w_in = (None, wb_in, wc_in)
@@ -112,12 +113,15 @@
                     )
                 near = z + up if v == 0 else z - up
                 far = z + 2 * up if v == 0 else z + up
+                last = z + (3 - v) * up
                 for cond, src in parts:
 
                     @pl.when(cond)
-                    def _(src=src, dst=dst, v=v, r=r, near=near, far=far):
+                    def _(src=src, dst=dst, v=v, r=r, near=near, far=far, last=last):
                         rc(src, dst, wz_s.at[a, v, r], wz_r.at[a, v, r], (d, near)).start()
                         rc(src, dst, wz_s2.at[a, v, r], wz_r.at[a, v, r], (d, far)).start()
+                        if a in DIRECT:
+                            rc(src, dst, wz_s3.at[v, r], wz_r.at[a, v, r], (d, last)).start()
 
     def w_copies(a, v):
         if a > 0:
@@ -142,6 +146,8 @@
                 ref = wg.at[a, uof(v), blk(r, p1, p2)]
                 n1_, n2_ = nbs(r)
                 cond = (zz == 3) if stage else ((zz == 1 - v) | (zz == 2))
+                if a in DIRECT:
+                    cond = zz != v
 
                 @pl.when(cond)
                 def _(ref=ref, v=v, r=r, n1_=n1_, n2_=n2_):
@@ -149,7 +155,7 @@
                     rc(ref, ref, wx_s.at[a, v, r, 0], wx_r.at[a, v, r, 0], n1_).start()
                     rc(ref, ref, wx_s.at[a, v, r, 1], wx_r.at[a, v, r, 1], n2_).start()
 
-                if not stage:
+                if not stage and a not in DIRECT:
 
                     @pl.when(zz == 2)
                     def _(ref=ref, v=v, r=r):
@@ -188,13 +194,15 @@
                 p1, p2 = pp(r)
                 ref = wg.at[a, uof(v), blk(r, p1, p2)]
 
-                @pl.when((zz == v) | (zz == 2))
+                @pl.when((zz == v) if a in DIRECT else ((zz == v) | (zz == 2)))
                 def _(ref=ref, v=v, r=r):
                     wait_send(ref, wz_s.at[a, v, r])
 
                 @pl.when(zz == v)
                 def _(ref=ref, v=v, r=r):
                     wait_send(ref, wz_s2.at[a, v, r])
+                    if a in DIRECT:
+                        wait_send(ref, wz_s3.at[v, r])
 
                 @pl.when(zz != v)
                 def _(ref=ref, v=v, r=r):
@@ -245,9 +253,6 @@
         return 0
 
     lax.fori_loop(0, 8, part, 0)
-    w_fwd(0, 0)
-    w_fwd(0, 1)
-
     for j in range(2):
         for h in range(2):
             zt = 2 * c + j
@@ -264,6 +269,8 @@
             def _(src=src, dst=dst, j=j, h=h, zt=zt):
                 rc(src, dst, x_s.at[j, h], x_r.at[z], (base + h, zt)).start()
 
+    w_fwd(0, 0)
+    w_fwd(0, 1)
     w_fwd2(0)
 
     def xrows(k, h):
@@ -355,6 +362,7 @@
 
         lax.fori_loop(0, 2, body, 0)
 
+    w_fwd(1, 0)
     w_start(2)
 
     def columns(h, s):
@@ -418,12 +426,11 @@
         lax.fori_loop(0, 2, back, 0)
 
     attend(0)
-    w_fwd(1, 0)
+    w_fwd(1, 1)
     attend(1)
-    w_fwd(1, 1)
     w_fwd2(1)
+    w_fwd(2, 0)
     attend(2)
-    w_fwd(2, 0)
 
     mine = 512 * c
     other = 512 - mine
@@ -472,7 +479,6 @@
 
     lax.fori_loop(0, 4, norm1, 0)
     share(flow, 0)
-    w_fwd(2, 1)
     w_done(1)
 
     for j in range(2):
@@ -698,18 +704,18 @@
         vb[0, pl.ds(6 + 2 * c + u, 1), cols] = ub
         return 0
 
-    lax.fori_loop(0, 6, dup, 0)
+    for u in range(2):
+        lax.fori_loop(3 * u, 3 * u + 3, dup, 0)
+        for n in range(3):
+            g[1, u, 256 * n : 256 * n + 256, :] = mm(
+                flow[:, 256 * n : 256 * n + 256], dg[:, 768 * u : 768 * u + 768], TN
+            ).astype(BF)
+        g_start(1, u)
     partial(
         lambda rows, cols: mm(dg[rows, 0:768], wg[1, 0, cols, :], NT)
         + mm(dg[rows, 768:1536], wg[1, 1, cols, :], NT),
         2,
     )
-    for u in range(2):
-        for n in range(3):
-            g[1, u, 256 * n : 256 * n + 256, :] = mm(
-                flow[:, 256 * n : 256 * n + 256], dg[:, 768 * u : 768 * u + 768], TN
-            ).astype(BF)
-        g_start(1, u)
 
     wait_send(dl.at[pl.ds(0, 512)], pe_s.at[5])
     def norm1b(m, carry):
@@ -826,7 +832,6 @@
     g_start(0, 1)
     for u in range(2):
         g_step3(1, u)
-    g_step4(2)
     bs = (b0, b1, b2)
     rest = jnp.zeros((1, 384), F32)
     for u in range(2):
@@ -858,23 +863,24 @@
         return 0
 
     lax.fori_loop(0, 4, gin, 0)
-    tok_send(gtok, o2, 1)
     v_add(0)
     v_send(1)
     g_step2(0, 0)
-    g_step5(2)
-    g_step3(0, 0)
     v_add(1)
     v_send(2)
-    g_step2(0, 1)
-    g_step6(2)
-    g_step4(1)
+    g_step3(0, 0)
     v_add(2)
     v_send(3)
-    g_step3(0, 1)
-    g_step5(1)
+    g_step2(0, 1)
     v_add(3)
     v_send(4)
+    g_step3(0, 1)
+    tok_send(gtok, o2, 1)
+    g_step4(2)
+    g_step4(1)
+    g_step5(2)
+    g_step5(1)
+    g_step6(2)
     g_step6(1)
     g_step4(0)
     g_step5(0)
@@ -969,7 +975,7 @@
             dma((2,)), dma((2,)), dma,
             dma((3,)), dma((2,)), dma,
             dma((2,)), dma((2,)), dma((2,)),
-            dma((3, 2, 2)), dma((3, 2, 2)), dma((3, 2, 2)),
+            dma((3, 2, 2)), dma((3, 2, 2)), dma((2, 2)), dma((3, 2, 2)),
             dma((3, 2, 2, 3)), dma((3, 2, 2, 3)), dma((4,)),
             dma((7,)), dma((7,)),
             dma((2, 2)), dma((2, 2)), dma((2,)),

time: 205 us -> 200 us (0.976)
  Pallas kernels: 204 us -> 199 us
    pallas_call x1, Pallas kernels: 197 us -> 192 us  [layer(): pl.pallas_call(kernel, out_shape=(jax.ShapeDtypeStruct((2, 256, 768), BF)...]
where the time goes in v3:
time: 200 us
  Pallas kernels  199 us (100%)
    pallas_call x1, Pallas kernels, layer(): pl.pallas_call(kernel, out_shape=(jax.ShapeDtypeStruct((2, 256, 768), BF)...  192 us
    pallas_call x1, Pallas kernels, finish(): pl.pallas_call(finish_kernel, out_shape=(S((256, 2, 768), BF), S((256, 2,...  7.15 us

profile of v3, /device:TPU:9, one launch (start us, length us, event | category | flops | bytes accessed | tf_op | source)
XLA Modules:
  0.0 200.0 jit_solution(4599725034763050863)
XLA Ops:
  0.7 192.0 %shard_map.263 = (bf16[2,256,768]{2,1,0:T(8,128)(2,1)}, bf16[2,256,768]{2,1,0:T(8,128)(2,1)}, bf16[768,768]{1,0:T(8,128)(2,1)}, bf16[768,768]{1,0:T(8,128)(2,1)}...) custom-call(bf16[256,2,768]{2,1,0:T(2,128)(2,1)} %x_in.1, s32[3,2,1024]{2,1,0:T(2,128)} %bitcast.10, ...), custom_call_target="tpu_custom_call" | custom-call | tf_op jit(solution)/shard_map/pallas_call | solution.py:926
  192.7 7.1 %shard_map.264 = (bf16[256,2,768]{2,1,0:T(2,128)(2,1)}, f32[256,2,768]{2,1,0:T(2,128)}, f32[576,768]{1,0:T(8,128)}, f32[192,768]{1,0:T(8,128)}, f32[768,768]{1,0...) custom-call(bf16[2,256,768]{2,1,0:T(8,128)(2,1)} %get-tuple-element., ...), custom_call_target="tpu_custom_call" | custom-call | tf_op jit(solution)/shard_map/pallas_call | solution.py:1060

commit v4 on v3

--- a/solution.py
+++ b/solution.py
@@ -34,7 +34,7 @@
     snd, rcv, op, fst, n1, rs1, flow, act, dg, dl, g, st1, st2, st3,
     rb, vb, vr,
     x_s, x_r, x_l, cx_s, cx_r, o_s, o_r, o_l, b_s, b_r, b_l, m_s, m_r, m_l,
-    wz_s, wz_s2, wz_s3, wz_r, wx_s, wx_r, w_l, pe_s, pe_r, t_s, t_r, t_l, v_s, v_r,
+    wz_s, wz_s2, wz_s3, wz_r, wx_s, wx_r, w_l, pe_s, pe_r, sh_s, sh_r, t_s, t_r, t_l, v_s, v_r,
     g1_s, g1_r, g2_s, g2_r, g3_s, g3_r, ag_s, ag_r, ag_l, ce_s, ce_r,
 ):
     w_in = (None, wb_in, wc_in)
@@ -276,23 +276,6 @@
     def xrows(k, h):
         return xall.at[pl.ds(pl.multiple_of(256 * k + 128 * h, 128), 128)]
 
-    for k in range(4):
-        ref = xrows(k, c)
-        loc = prim & (z == k)
-
-        @pl.when(loc)
-        def _(ref=ref):
-            lc(ref, ref, x_l).wait()
-
-        @pl.when(jnp.logical_not(loc))
-        def _(ref=ref, k=k):
-            wait_recv(ref, x_r.at[k])
-
-        rc(ref, ref, cx_s.at[k], cx_r.at[k], (sib, z)).start()
-    w_start(1)
-    for k in range(4):
-        wait_recv(xrows(k, 1 - c), cx_r.at[k])
-
     for u in range(2):
         loc = prim & (zj == u)
 
@@ -336,6 +319,23 @@
             wq[384 * i + 64 * n : 384 * i + 64 * n + 64, :] = wg[0, u, rows, :]
         for n, (u, rows) in enumerate((place(2 * i + 1, 3), place(2 * i, 3))):
             wo[128 * i + 64 * n : 128 * i + 64 * n + 64, :] = wg[0, u, rows, :]
+
+    for k in range(4):
+        ref = xrows(k, c)
+        loc = prim & (z == k)
+
+        @pl.when(loc)
+        def _(ref=ref):
+            lc(ref, ref, x_l).wait()
+
+        @pl.when(jnp.logical_not(loc))
+        def _(ref=ref, k=k):
+            wait_recv(ref, x_r.at[k])
+
+        rc(ref, ref, cx_s.at[k], cx_r.at[k], (sib, z)).start()
+    w_start(1)
+    for k in range(4):
+        wait_recv(xrows(k, 1 - c), cx_r.at[k])
 
     def bq(i):
         nil = jnp.zeros((1, 64), F32)
@@ -539,6 +539,8 @@
         fst[rr, :] = d2
         dlo = d2.astype(BF)
         dl[at(mine, m, 128), :] = dlo
+        piece_ = dl.at[at(mine, m, 128)]
+        rc(piece_, piece_, sh_s.at[m], sh_r.at[m], (sib, z)).start()
         return (
             sgain + jnp.sum(dout * nv, axis=0, keepdims=True),
             sshift + jnp.sum(dout, axis=0, keepdims=True),
@@ -546,7 +548,6 @@
         )
 
     sg, ss, db = lax.fori_loop(0, 4, norm2, (ones8, ones8, ones8))
-    share(dl, 1)
     vb[0, 0:1, :] = sg
     vb[0, 1:2, :] = ss
     vb[0, 2:3, :] = db
@@ -684,7 +685,8 @@
                 def _(u=u, r=r):
                     wait_send(st2.at[a, u, r], g3_s.at[a, u, r])
 
-    shared(dl, 1)
+    for m in range(4):
+        wait_recv(dl.at[at(other, m, 128)], sh_r.at[m])
 
     for u in range(2):
         for n in range(3):
@@ -717,7 +719,8 @@
         2,
     )
 
-    wait_send(dl.at[pl.ds(0, 512)], pe_s.at[5])
+    for m in range(4):
+        wait_send(dl.at[pl.ds(0, 128)], sh_s.at[m])
     def norm1b(m, carry):
         fg, fs, ob = carry
         rr = rows_of(m, 128)
@@ -977,7 +980,7 @@
             dma((2,)), dma((2,)), dma((2,)),
             dma((3, 2, 2)), dma((3, 2, 2)), dma((2, 2)), dma((3, 2, 2)),
             dma((3, 2, 2, 3)), dma((3, 2, 2, 3)), dma((4,)),
-            dma((7,)), dma((7,)),
+            dma((7,)), dma((7,)), dma((4,)), dma((4,)),
             dma((2, 2)), dma((2, 2)), dma((2,)),
             dma((5,)), dma((5,)),
             dma((3, 2, 2)), dma((3, 2, 2)), dma((3, 2, 2)), dma((3, 2, 2)),

time: 200 us -> 198 us (0.990)
  Pallas kernels: 199 us -> 197 us
where the time goes in v4:
time: 198 us
  Pallas kernels  197 us (99%)
    pallas_call x1, Pallas kernels, layer(): pl.pallas_call(kernel, out_shape=(jax.ShapeDtypeStruct((2, 256, 768), BF)...  190 us
    pallas_call x1, Pallas kernels, finish(): pl.pallas_call(finish_kernel, out_shape=(S((256, 2, 768), BF), S((256, 2,...  7.15 us

profile of v4, /device:TPU:9, one launch (start us, length us, event | category | flops | bytes accessed | tf_op | source)
XLA Modules:
  0.0 198.2 jit_solution(18109453970694003358)
XLA Ops:
  0.7 190.2 %shard_map.263 = (bf16[2,256,768]{2,1,0:T(8,128)(2,1)}, bf16[2,256,768]{2,1,0:T(8,128)(2,1)}, bf16[768,768]{1,0:T(8,128)(2,1)}, bf16[768,768]{1,0:T(8,128)(2,1)}...) custom-call(bf16[256,2,768]{2,1,0:T(2,128)(2,1)} %x_in.1, s32[3,2,1024]{2,1,0:T(2,128)} %bitcast.10, ...), custom_call_target="tpu_custom_call" | custom-call | tf_op jit(solution)/shard_map/pallas_call | solution.py:929
  190.8 7.1 %shard_map.264 = (bf16[256,2,768]{2,1,0:T(2,128)(2,1)}, f32[256,2,768]{2,1,0:T(2,128)}, f32[576,768]{1,0:T(8,128)}, f32[192,768]{1,0:T(8,128)}, f32[768,768]{1,0...) custom-call(bf16[2,256,768]{2,1,0:T(8,128)(2,1)} %get-tuple-element., ...), custom_call_target="tpu_custom_call" | custom-call | tf_op jit(solution)/shard_map/pallas_call | solution.py:1063
